TPU v7x, 512 devices: a whole 4x4x16 slice. The times are simulated.
512 devices in a mesh: slab: 64 (over z, y), head: 8 (over x, core).
Axes of the slice: x: 4, y: 4, z: 16, core: 2. Of those that a mesh axis runs over, the one named last changes fastest.
Arguments:
- video_token_state: bfloat16 [24576, 3072], P('slab'), may hold values from -6 to 6
- text_tokens: bfloat16 [128, 3072], replicated, may hold values from -6 to 6
- text_mask: int32 [128], replicated, may hold values from 0 to 1, as said below
- head_window: int32 [16, 2], replicated, may hold values from 0 to 1, as said below
- video_query_weight: bfloat16 [3072, 2048], P('slab', 'head'), may hold values from -0.109375 to 0.109375
- video_key_weight: bfloat16 [3072, 2048], P('slab', 'head'), may hold values from -0.109375 to 0.109375
- video_value_weight: bfloat16 [3072, 2048], P('slab', 'head'), may hold values from -0.109375 to 0.109375
- wout_video: bfloat16 [2048, 3072], P('head', 'slab'), may hold values from -0.125 to 0.125
- wquery_text: bfloat16 [3072, 2048], P('slab', 'head'), may hold values from -0.109375 to 0.109375
- wkey_text: bfloat16 [3072, 2048], P('slab', 'head'), may hold values from -0.109375 to 0.109375
- wvalue_text: bfloat16 [3072, 2048], P('slab', 'head'), may hold values from -0.109375 to 0.109375
- video_query_gain: float32 [128], replicated, may hold values from 1.25 to 2.5
- video_key_gain: float32 [128], replicated, may hold values from 1.25 to 2.5
- qgain_text: float32 [128], replicated, may hold values from 1.25 to 2.5
- kgain_text: float32 [128], replicated, may hold values from 1.25 to 2.5
Outputs:
- video_out: bfloat16 [24576, 3072], P(('slab', 'head'))
- text_attn: bfloat16 [128, 2048], P(None, 'head')
Inputs may be any that keep to these rules, and one draw needn't show every extreme that they name: `text_mask`: the ones form a prefix: the first 16 text tokens are always real and the last one never is. `head_window`: each of the values 0 and 1 is taken by some head in each of the two columns.
All inputs are finite; a program needn't handle non-finite values.
Results may differ from a plain program's by a relative error of at most 0.019.
Values may be sent and summed in bfloat16 or wider, within the bound.
A program may use at most 64 MiB of HBM per device.

v0:
```python
import math

import jax
import jax.numpy as jnp
from jax import lax
from jax.sharding import PartitionSpec as P

HEAD_SIZE = 128
COLUMN_TILES = 8


norm_eps = 1e-06


def from_behind(array, axis, by):
    count = lax.axis_size(axis)
    pairs = [(i, i + by) for i in range(count) if 0 <= i + by < count]
    return lax.ppermute(array, axis, pairs)


def layer_normalize(token_rows):
    values = token_rows.astype(jnp.float32)
    center = values - jnp.mean(values, axis=-1, keepdims=True)
    spread = jnp.mean(center * center, axis=-1, keepdims=True)
    return (center * lax.rsqrt(spread + norm_eps)).astype(jnp.bfloat16)


def per_head_norm(projected, gain):
    row_count = projected.shape[0]
    per_head = projected.reshape(row_count, -1, gain.shape[0])
    mean_square = jnp.mean(per_head * per_head, axis=-1, keepdims=True)
    return (
        (per_head * lax.rsqrt(mean_square + norm_eps) * gain)
        .reshape(row_count, -1)
        .astype(jnp.bfloat16)
    )


def merge_into(totals, pieces, sources):
    result = []
    for running, segment, source in zip(totals, pieces, sources):
        result.append(jnp.dot(source, segment, preferred_element_type=jnp.float32))
    return tuple(result)


def on_device(
    video_token_state,
    text_tokens,
    text_mask,
    head_window,
    video_query_weight,
    video_key_weight,
    video_value_weight,
    wout_video,
    wquery_text,
    wkey_text,
    wvalue_text,
    video_query_gain,
    video_key_gain,
    qgain_text,
    kgain_text,
):
    slab_count = lax.axis_size("slab")
    slab_place = lax.axis_index("slab")
    head_place = lax.axis_index("head")
    tile_row_span = slab_count // COLUMN_TILES
    band_row = slab_place // COLUMN_TILES
    band_col = slab_place % COLUMN_TILES
    shard_heads = video_query_weight.shape[1] // HEAD_SIZE
    model_width = shard_heads * HEAD_SIZE
    score_scale = 1.0 / math.sqrt(HEAD_SIZE)
    video_normed = layer_normalize(video_token_state)
    text_normed = layer_normalize(text_tokens)
    token_count = video_normed.shape[0]
    txt_count = text_normed.shape[0]
    video_empty = jnp.zeros((token_count, model_width), jnp.float32)
    text_empty = jnp.zeros((txt_count, model_width), jnp.float32)
    sources = (video_normed, video_normed, video_normed, text_normed, text_normed, text_normed)
    video_query, video_keys, video_values, text_query, text_keys, text_values = merge_into(
        (video_empty, video_empty, video_empty, text_empty, text_empty, text_empty),
        (
            lax.all_gather(video_query_weight, "slab", axis=0, tiled=True),
            lax.all_gather(video_key_weight, "slab", axis=0, tiled=True),
            lax.all_gather(video_value_weight, "slab", axis=0, tiled=True),
            lax.all_gather(wquery_text, "slab", axis=0, tiled=True),
            lax.all_gather(wkey_text, "slab", axis=0, tiled=True),
            lax.all_gather(wvalue_text, "slab", axis=0, tiled=True),
        ),
        sources,
    )
    video_query = per_head_norm(video_query, video_query_gain)
    video_keys = per_head_norm(video_keys, video_key_gain)
    video_values = video_values.astype(jnp.bfloat16)
    text_query = per_head_norm(text_query, qgain_text)
    text_keys = per_head_norm(text_keys, kgain_text)
    text_values = text_values.astype(jnp.bfloat16)
    stacked_rows = jnp.stack([video_keys, video_values])
    gathered = []
    for row_move in (-1, 0, 1):
        for col_move in (-1, 0, 1):
            if row_move == 0 and col_move == 0:
                gathered.append(stacked_rows)
            else:
                gathered.append(
                    from_behind(stacked_rows, "slab", -(row_move * COLUMN_TILES + col_move))
                )
    bordered = jnp.concatenate(gathered, axis=1)
    window = lax.dynamic_slice_in_dim(head_window, head_place * shard_heads, shard_heads, 0)
    row_step = jnp.repeat(jnp.arange(-1, 2, dtype=jnp.int32), 3)
    col_step = jnp.tile(jnp.arange(-1, 2, dtype=jnp.int32), 3)
    inside = (
        (band_row + row_step >= 0)
        & (band_row + row_step < tile_row_span)
        & (band_col + col_step >= 0)
        & (band_col + col_step < COLUMN_TILES)
    )
    reach = (
        (jnp.abs(row_step)[None, :] <= window[:, 0, None])
        & (jnp.abs(col_step)[None, :] <= window[:, 1, None])
        & inside[None, :]
    )
    allowed = jnp.repeat(reach, token_count, axis=1)
    text_live = text_mask > 0
    query_heads = video_query.reshape(token_count, shard_heads, HEAD_SIZE)
    near_keys = bordered[0].reshape(9 * token_count, shard_heads, HEAD_SIZE)
    near_values = bordered[1].reshape(9 * token_count, shard_heads, HEAD_SIZE)
    text_key_heads = text_keys.reshape(txt_count, shard_heads, HEAD_SIZE)
    text_value_heads = text_values.reshape(txt_count, shard_heads, HEAD_SIZE)
    weights = jnp.where(
        allowed[:, None, :],
        jnp.exp(
            jnp.einsum("qhd,khd->hqk", query_heads, near_keys, preferred_element_type=jnp.float32)
            * score_scale
        ),
        0.0,
    )
    text_weights = jnp.where(
        text_live[None, None, :],
        jnp.exp(
            jnp.einsum(
                "qhd,khd->hqk", query_heads, text_key_heads, preferred_element_type=jnp.float32
            )
            * score_scale
        ),
        0.0,
    )
    denominator = jnp.sum(weights, axis=2) + jnp.sum(text_weights, axis=2)
    numerator = jnp.einsum(
        "hqk,khd->qhd",
        weights.astype(jnp.bfloat16),
        near_values,
        preferred_element_type=jnp.float32,
    )
    numerator = numerator + jnp.einsum(
        "hqk,khd->qhd",
        text_weights.astype(jnp.bfloat16),
        text_value_heads,
        preferred_element_type=jnp.float32,
    )
    video_attn = (
        (numerator / jnp.transpose(denominator)[:, :, None])
        .reshape(token_count, model_width)
        .astype(jnp.bfloat16)
    )
    text_query_heads = text_query.reshape(txt_count, shard_heads, HEAD_SIZE)
    tile_own_keys = video_keys.reshape(token_count, shard_heads, HEAD_SIZE)
    own_values = video_values.reshape(token_count, shard_heads, HEAD_SIZE)
    far_weights = jnp.exp(
        jnp.einsum(
            "qhd,khd->hqk", text_query_heads, tile_own_keys, preferred_element_type=jnp.float32
        )
        * score_scale
    )
    far_numerator = jnp.einsum(
        "hqk,khd->qhd",
        far_weights.astype(jnp.bfloat16),
        own_values,
        preferred_element_type=jnp.float32,
    )
    far_denominator = jnp.sum(far_weights, axis=2)
    far_numerator, far_denominator = lax.psum((far_numerator, far_denominator), "slab")
    self_weights = jnp.where(
        text_live[None, None, :],
        jnp.exp(
            jnp.einsum(
                "qhd,khd->hqk", text_query_heads, text_key_heads, preferred_element_type=jnp.float32
            )
            * score_scale
        ),
        0.0,
    )
    text_numerator = far_numerator + jnp.einsum(
        "hqk,khd->qhd",
        self_weights.astype(jnp.bfloat16),
        text_value_heads,
        preferred_element_type=jnp.float32,
    )
    text_denominator = far_denominator + jnp.sum(self_weights, axis=2)
    text_attn = (
        (text_numerator / jnp.transpose(text_denominator)[:, :, None])
        .reshape(txt_count, model_width)
        .astype(jnp.bfloat16)
    )
    out_weights = lax.all_gather(wout_video, "slab", axis=1, tiled=True)
    video_out = lax.psum_scatter(
        jnp.dot(video_attn, out_weights, preferred_element_type=jnp.float32).astype(jnp.bfloat16),
        "head",
        scatter_dimension=0,
        tiled=True,
    )
    return (video_out, text_attn)


def solution(mesh):
    return jax.shard_map(
        on_device,
        mesh=mesh,
        in_specs=(
            P("slab", None),
            P(),
            P(),
            P(),
            P("slab", "head"),
            P("slab", "head"),
            P("slab", "head"),
            P("head", "slab"),
            P("slab", "head"),
            P("slab", "head"),
            P("slab", "head"),
            P(),
            P(),
            P(),
            P(),
        ),
        out_specs=(P(("slab", "head"), None), P(None, "head")),
        check_vma=False,
    )
```

profile of v0, /device:TPU:6, one launch (start us, length us, event | category | flops | bytes accessed | tf_op | source)
XLA Modules:
  0.0 1328.0 jit_solution(16252424175216712812)
XLA Ops:
  11.2 0.7 all-gather.18.cloned.1.call-update
  12.0 2.1 convert_reduce_fusion
  14.0 0.8 fusion.9
  14.9 2.4 fusion.10
  20.4 135.6 %all-gather.8.cloned.1.call-done = bf16[3072,256]{1,0:T(8,128)(2,1)} async-done(((bf16[48,256]{1,0:T(8,128)(2,1)}), bf16[3072,256]{1,0:T(8,128)(2,1)}) %all-gather.8.cloned.1.call-update) | async-done | bytes 1572880 | tf_op jit(solution)/shard_map/all_gather | solution.py:83
  156.0 3.2 bitcast_reduce_fusion.1
  159.3 136.0 %all-gather.10.cloned.1.call-done = bf16[3072,256]{1,0:T(8,128)(2,1)} async-done(((bf16[48,256]{1,0:T(8,128)(2,1)}), bf16[3072,256]{1,0:T(8,128)(2,1)}) %all-gather.10.cloned.1.call-update) | async-done | bytes 1572880 | tf_op jit(solution)/shard_map/all_gather | solution.py:84
  295.2 2.4 convolution_convert_fusion.1
  297.7 0.8 pad_maximum_fusion
  298.5 3.7 collective-permute-start
  302.2 4.5 collective-permute-start.1
  306.7 6.6 collective-permute-start.2
  313.4 2.0 collective-permute-start.3
  315.4 1.3 collective-permute-start.4
  316.7 133.2 %all-gather.16.cloned.1.call-done = bf16[3072,256]{1,0:T(8,128)(2,1)} async-done(((bf16[48,256]{1,0:T(8,128)(2,1)}), bf16[3072,256]{1,0:T(8,128)(2,1)}) %all-gather.16.cloned.1.call-update) | async-done | bytes 1572880 | tf_op jit(solution)/shard_map/all_gather | solution.py:86
  450.0 2.5 fusion.69
  452.5 1.6 mul.197
  454.1 134.9 %all-gather.20.cloned.1.call-done = bf16[3072,256]{1,0:T(8,128)(2,1)} async-done(((bf16[48,256]{1,0:T(8,128)(2,1)}), bf16[3072,256]{1,0:T(8,128)(2,1)}) %all-gather.20.cloned.1.call-update) | async-done | bytes 1572880 | tf_op jit(solution)/shard_map/all_gather | solution.py:85
  589.1 2.5 fusion.71
  591.6 1.6 mul.208
  593.2 1.7 reduce_sum.114
  595.0 1.7 reduce_sum.117
  596.7 131.4 %all-gather.14.cloned.1.call-done = bf16[3072,256]{1,0:T(8,128)(2,1)} async-done(((bf16[48,256]{1,0:T(8,128)(2,1)}), bf16[3072,256]{1,0:T(8,128)(2,1)}) %all-gather.14.cloned.1.call-update) | async-done | bytes 1572880 | tf_op jit(solution)/shard_map/all_gather | solution.py:87
  728.2 2.5 convolution_convert_fusion.2
  730.7 0.9 copy.68
  731.6 135.6 %all-gather.12.cloned.1.call-done = bf16[3072,256]{1,0:T(8,128)(2,1)} async-done(((bf16[48,256]{1,0:T(8,128)(2,1)}), bf16[3072,256]{1,0:T(8,128)(2,1)}) %all-gather.12.cloned.1.call-update) | async-done | bytes 1572880 | tf_op jit(solution)/shard_map/all_gather | solution.py:82
  867.3 2.5 bitcast_reduce_fusion
  871.2 0.9 convolution_bitcast_fusion
  872.2 1.3 collective-permute-start.5
  873.5 1.0 constant_dynamic-update-slice_fusion.8
  874.5 1.3 collective-permute-start.6
  875.8 1.1 constant_dynamic-update-slice_fusion.7
  876.9 1.5 collective-permute-start.7
  878.4 1.1 constant_dynamic-update-slice_fusion.6
  879.5 1.1 constant_dynamic-update-slice_fusion.5
  880.6 1.1 constant_dynamic-update-slice_fusion.3
  881.7 4.3 collective-permute-done.5
  886.0 11.0 collective-permute-done.6
  897.1 23.0 %collective-permute-done.7 = bf16[2,384,256]{1,2,0:T(8,128)(2,1)S(1)} collective-permute-done((bf16[2,384,256]{1,2,0:T(8,128)(2,1)}, bf16[2,384,256]{1,2,0:T(8,128)(2,1)S(1)}, u32[]{:S(2)}, u32[]{:S(2)}) %collective-permute-start.7) | collective-permute-done | bytes 393248 | tf_op jit(solution)/shard_map/ppermute | solution.py:18
  920.9 2.6 fusion
  923.5 1.7 fusion.32
  925.2 99.8 %all-gather.18.cloned.1.call-done = bf16[256,3072]{0,1:T(8,128)(2,1)} async-done(((bf16[256,48]{0,1:T(8,128)(2,1)}), bf16[256,3072]{0,1:T(8,128)(2,1)}) %all-gather.18.cloned.1.call-update) | async-done | bytes 1572880 | tf_op jit(solution)/shard_map/all_gather | solution.py:204
  1025.0 3.7 convolution_convert_fusion
  1028.7 141.3 %psum.15 = f32[2,128]{1,0:T(2,128)S(1)} all-reduce(f32[2,128]{1,0:T(2,128)S(1)} %get-tuple-element.24), channel_id=1, replica_groups=mesh['slab'=64,'head'=8] {'slab'}, use_global_device_ids=true, to_apply=%region_13.14 | all-reduce | flops 256 | bytes 2048 | tf_op jit(solution)/shard_map/psum | solution.py:181
  1170.2 114.9 %all-reduce.2.cloned.1.call-done = f32[128,2,128]{0,2,1:T(8,128)} async-done(((f32[128,2,128]{0,2,1:T(8,128)}), f32[128,2,128]{0,2,1:T(8,128)}) %all-reduce.2.cloned.1.call-update) | async-done | bytes 131088 | tf_op jit(solution)/shard_map/psum | solution.py:181
  1285.1 1.1 fusion.28
  1286.2 0.7 copy.61
  1286.9 34.5 %reduce-scatter.2.cloned.1.call-done = bf16[48,3072]{1,0:T(8,128)(2,1)} async-done(((bf16[384,3072]{1,0:T(8,128)(2,1)}), bf16[48,3072]{1,0:T(8,128)(2,1)}) %reduce-scatter.2.cloned.1.call-update) | async-done | bytes 294928 | tf_op jit(solution)/shard_map/reduce_scatter | solution.py:205
  (101 shorter events, 9.7 us)
Async XLA Ops:
  7.2 10.4 copy-start
  7.2 6.9 copy-start.1
  7.2 148.8 %all-gather.8.cloned.1.call-start = ((), (), s32[]{:S(2)}) async-start(), calls=%async_computation.1 | async-start | bytes 1597440 | tf_op jit(solution)/shard_map/all_gather | solution.py:83
  7.9 287.3 %all-gather.10.cloned.1.call-start = ((), (), s32[]{:S(2)}) async-start(), calls=%async_computation.2 | async-start | bytes 1597440 | tf_op jit(solution)/shard_map/all_gather | solution.py:84
  8.7 441.3 %all-gather.16.cloned.1.call-start = ((), (), s32[]{:S(2)}) async-start(), calls=%async_computation.5 | async-start | bytes 1597440 | tf_op jit(solution)/shard_map/all_gather | solution.py:86
  9.4 579.7 %all-gather.20.cloned.1.call-start = ((), (), s32[]{:S(2)}) async-start(), calls=%async_computation.8 | async-start | bytes 1597440 | tf_op jit(solution)/shard_map/all_gather | solution.py:85
  10.0 718.2 %all-gather.14.cloned.1.call-start = ((), (), s32[]{:S(2)}) async-start(), calls=%async_computation.4 | async-start | bytes 1597440 | tf_op jit(solution)/shard_map/all_gather | solution.py:87
  10.6 856.7 %all-gather.12.cloned.1.call-start = ((), (), s32[]{:S(2)}) async-start(), calls=%async_computation.3 | async-start | bytes 1597440 | tf_op jit(solution)/shard_map/all_gather | solution.py:82
  11.1 1013.8 %all-gather.18.cloned.1.call-start = ((), (), s32[]{:S(2)}) async-start(), calls=%async_computation.6 | async-start | bytes 1597440 | tf_op jit(solution)/shard_map/all_gather | solution.py:204
  11.9 1273.2 %all-reduce.2.cloned.1.call-start = ((), (), s32[]{:S(2)}) async-start(), calls=%async_computation.9 | async-start | bytes 262144 | tf_op jit(solution)/shard_map/psum | solution.py:181
  14.8 2.5 copy-start.10
  14.8 3.8 copy-start.11
  14.8 3.8 copy-start.3
  14.8 5.0 copy-start.12
  14.9 4.9 copy-start.13
  14.9 4.9 copy-start.14
  18.8 140.3 %copy-start.9 = (f32[128]{0:T(128)}, f32[128]{0:T(128)S(1)}, u32[]{:S(2)}) copy-start(f32[128]{0:T(128)S(1)} %broadcast_multiply_fusion.1) | copy-start | bytes 1540
  20.4 274.8 %copy-start.2 = (bf16[384,3072]{1,0:T(8,128)(2,1)S(1)}, bf16[384,3072]{1,0:T(8,128)(2,1)}, u32[]{:S(2)}) copy-start(bf16[384,3072]{1,0:T(8,128)(2,1)} %fusion.10) | copy-start | bytes 7077892
  298.5 573.7 %collective-permute-start = (bf16[2,384,256]{1,2,0:T(8,128)(2,1)}, bf16[2,384,256]{1,2,0:T(8,128)(2,1)}, u32[]{:S(2)}, u32[]{:S(2)}) collective-permute-start(bf16[2,384,256]{1,2,0:T(8,128)(2,1)} %pad_maximum_fusion), channel_id=1, source_target_pairs={{0,72},{8,80},{16,88},{24,96},{32,104},{40,112},{48,120},{56,128},... | collective-permute-start | bytes 1179656 | tf_op jit(solution)/shard_map/ppermute | solution.py:18
  302.2 572.3 %collective-permute-start.1 = (bf16[2,384,256]{1,2,0:T(8,128)(2,1)}, bf16[2,384,256]{1,2,0:T(8,128)(2,1)}, u32[]{:S(2)}, u32[]{:S(2)}) collective-permute-start(bf16[2,384,256]{1,2,0:T(8,128)(2,1)} %pad_maximum_fusion), channel_id=1, source_target_pairs={{0,64},{8,72},{16,80},{24,88},{32,96},{40,104},{48,112},{56,120},{... | collective-permute-start | bytes 1179656 | tf_op jit(solution)/shard_map/ppermute | solution.py:18
  306.7 570.2 %collective-permute-start.2 = (bf16[2,384,256]{1,2,0:T(8,128)(2,1)}, bf16[2,384,256]{1,2,0:T(8,128)(2,1)}, u32[]{:S(2)}, u32[]{:S(2)}) collective-permute-start(bf16[2,384,256]{1,2,0:T(8,128)(2,1)} %pad_maximum_fusion), channel_id=1, source_target_pairs={{0,56},{8,64},{16,72},{24,80},{32,88},{40,96},{48,104},{56,112},{6... | collective-permute-start | bytes 1179656 | tf_op jit(solution)/shard_map/ppermute | solution.py:18
  313.4 566.1 %collective-permute-start.3 = (bf16[2,384,256]{1,2,0:T(8,128)(2,1)}, bf16[2,384,256]{1,2,0:T(8,128)(2,1)}, u32[]{:S(2)}, u32[]{:S(2)}) collective-permute-start(bf16[2,384,256]{1,2,0:T(8,128)(2,1)} %pad_maximum_fusion), channel_id=1, source_target_pairs={{0,8},{8,16},{16,24},{24,32},{32,40},{40,48},{48,56},{56,64},{64,7... | collective-permute-start | bytes 1179656 | tf_op jit(solution)/shard_map/ppermute | solution.py:18
  315.4 565.2 %collective-permute-start.4 = (bf16[2,384,256]{1,2,0:T(8,128)(2,1)}, bf16[2,384,256]{1,2,0:T(8,128)(2,1)}, u32[]{:S(2)}, u32[]{:S(2)}) collective-permute-start(bf16[2,384,256]{1,2,0:T(8,128)(2,1)} %pad_maximum_fusion), channel_id=1, source_target_pairs={{8,0},{16,8},{24,16},{32,24},{40,32},{48,40},{56,48},{64,56},{72,6... | collective-permute-start | bytes 1179656 | tf_op jit(solution)/shard_map/ppermute | solution.py:18
  731.6 138.3 %copy-start.4 = (f32[128,2]{1,0:T(8,128)S(1)}, f32[128,2]{1,0:T(8,128)}, u32[]{:S(2)}) copy-start(f32[128,2]{1,0:T(8,128)} %reduce_sum.114) | copy-start | bytes 3076
  731.6 138.3 %copy-start.5 = (f32[128,2]{1,0:T(8,128)S(1)}, f32[128,2]{1,0:T(8,128)}, u32[]{:S(2)}) copy-start(f32[128,2]{1,0:T(8,128)} %reduce_sum.117) | copy-start | bytes 3076
  731.6 138.8 %copy-start.6 = (f32[128,256]{1,0:T(8,128)S(1)}, f32[128,256]{1,0:T(8,128)}, u32[]{:S(2)}) copy-start(f32[128,256]{1,0:T(8,128)} %get-tuple-element.15) | copy-start | bytes 393220
  867.3 3.1 copy-start.7
  867.3 3.2 copy-start.15
  872.1 449.3 %reduce-scatter.2.cloned.1.call-start = ((), (), s32[]{:S(2)}) async-start(), calls=%async_computation.7 | async-start | bytes 2654208 | tf_op jit(solution)/shard_map/reduce_scatter | solution.py:205
  872.2 13.8 %collective-permute-start.5 = (bf16[2,384,256]{1,2,0:T(8,128)(2,1)}, bf16[2,384,256]{1,2,0:T(8,128)(2,1)S(1)}, u32[]{:S(2)}, u32[]{:S(2)}) collective-permute-start(bf16[2,384,256]{1,2,0:T(8,128)(2,1)} %pad_maximum_fusion), channel_id=1, source_target_pairs={{56,0},{64,8},{72,16},{80,24},{88,32},{96,40},{104,48},{112,56},{1... | collective-permute-start | bytes 1179656 | tf_op jit(solution)/shard_map/ppermute | solution.py:18
  874.5 22.5 %collective-permute-start.6 = (bf16[2,384,256]{1,2,0:T(8,128)(2,1)}, bf16[2,384,256]{1,2,0:T(8,128)(2,1)S(1)}, u32[]{:S(2)}, u32[]{:S(2)}) collective-permute-start(bf16[2,384,256]{1,2,0:T(8,128)(2,1)} %pad_maximum_fusion), channel_id=1, source_target_pairs={{64,0},{72,8},{80,16},{88,24},{96,32},{104,40},{112,48},{120,56},{... | collective-permute-start | bytes 1179656 | tf_op jit(solution)/shard_map/ppermute | solution.py:18
  876.9 43.2 %collective-permute-start.7 = (bf16[2,384,256]{1,2,0:T(8,128)(2,1)}, bf16[2,384,256]{1,2,0:T(8,128)(2,1)S(1)}, u32[]{:S(2)}, u32[]{:S(2)}) collective-permute-start(bf16[2,384,256]{1,2,0:T(8,128)(2,1)} %pad_maximum_fusion), channel_id=1, source_target_pairs={{72,0},{80,8},{88,16},{96,24},{104,32},{112,40},{120,48},{128,56},... | collective-permute-start | bytes 1179656 | tf_op jit(solution)/shard_map/ppermute | solution.py:18
  920.2 0.7 copy-start.8
  1025.0 145.0 %copy-start.16 = (pred[128]{0:T(512)(128)(4,1)S(1)}, pred[128]{0:T(512)(128)(4,1)}, u32[]{:S(2)}) copy-start(pred[128]{0:T(512)(128)(4,1)} %broadcast_compare_fusion) | copy-start | bytes 388
Sparse Core Ops, SparseCore 0:
  11.0 144.9 all-gather.7
  158.9 136.2 all-gather.9
  298.2 151.7 all-gather.15
  452.8 136.2 all-gather.19
  591.9 136.2 all-gather.13
  731.0 136.2 all-gather.11
  870.2 154.7 all-gather.17
  1028.4 256.6 all-reduce.1
  1288.5 32.8 reduce-scatter.1
where the time goes:
time: 1330 us
  waiting for transfers between devices  1100 us (83%)
  blocking collectives  141 us (11%)
  matrix products  26.5 us (2%)
  starting transfers between devices  22.6 us (2%)
  between operations  14.3 us (1%)
    psum x1, blocking collectives, on_device(): lax.psum((far_numerator, far_denominator), 'slab')  141 us
    all_gather x1, waiting for transfers between devices, on_device(): lax.all_gather(video_value_weight, 'slab', axis=0, tiled=True)  136 us
    all_gather x1, waiting for transfers between devices, on_device(): lax.all_gather(video_query_weight, 'slab', axis=0, tiled=True)  136 us
    all_gather x1, waiting for transfers between devices, on_device(): lax.all_gather(video_key_weight, 'slab', axis=0, tiled=True)  136 us
    all_gather x1, waiting for transfers between devices, on_device(): lax.all_gather(wquery_text, 'slab', axis=0, tiled=True)  135 us
    all_gather x1, waiting for transfers between devices, on_device(): lax.all_gather(wkey_text, 'slab', axis=0, tiled=True)  133 us
    all_gather x1, waiting for transfers between devices, on_device(): lax.all_gather(wvalue_text, 'slab', axis=0, tiled=True)  131 us
    psum x1, waiting for transfers between devices, on_device(): lax.psum((far_numerator, far_denominator), 'slab')  115 us
  transfers between devices with their start and end apart: 17, of which 12 were waited for; matrix products, arithmetic and copies ran while one was open for 4% of the time, Pallas kernels for 0%

commit v1 on v0

v1 whole, which is shorter than its diff:
```python
import functools
import math

import jax
import jax.numpy as jnp
from jax import lax
from jax.experimental import pallas as pl
from jax.experimental.pallas import tpu as pltpu
from jax.sharding import PartitionSpec as P

HEAD_SIZE = 128
COLUMN_TILES = 8
Y = 4
MIB = 1 << 20
LANES = 128
VMEM = pltpu.VMEM
DMA = pltpu.SemaphoreType.DMA

norm_eps = 1e-06


def mod(a, n):
    return lax.rem(a, jnp.int32(n))


def remote(src, dst, send, recv, **device):
    return pltpu.make_async_remote_copy(
        src_ref=src, dst_ref=dst, send_sem=send, recv_sem=recv,
        device_id=device, device_id_type=pl.DeviceIdType.MESH,
    )


def greet(slabs=(), heads=()):
    barrier = pltpu.get_barrier_semaphore()
    for slab in slabs:
        pl.semaphore_signal(barrier, 1, device_id={"slab": slab}, device_id_type=pl.DeviceIdType.MESH)
    for head in heads:
        pl.semaphore_signal(barrier, 1, device_id={"head": head}, device_id_type=pl.DeviceIdType.MESH)
    return barrier


def when(condition, step):
    if isinstance(condition, bool):
        if condition:
            step()
    else:
        pl.when(condition)(step)


def hello_slab(z, y, nz):
    barrier = pltpu.get_barrier_semaphore()

    def greet_one(slab):
        pl.semaphore_signal(barrier, 1, device_id={"slab": slab}, device_id_type=pl.DeviceIdType.MESH)

    for d in range(1, Y):
        greet_one(z * Y + mod(y + d, Y))

    def body(d, carry):
        greet_one(mod(z + d, nz) * Y + y)
        return carry

    lax.fori_loop(1, nz, body, 0)
    return barrier, Y - 1 + nz - 1


class SlabSum:
    @staticmethod
    def scratch(block):
        owners, nz, rows, lanes = block.shape
        return [
            VMEM((Y, nz, rows, lanes), block.dtype),
            VMEM((nz, rows, lanes), block.dtype),
            VMEM((nz, rows, lanes), block.dtype),
            DMA((2, 2, Y)),
            DMA((2, 2, nz)),
        ]

    def __init__(self, part, out, scratch):
        self.part, self.out = part, out
        self.from_y, self.sum_y, self.from_z, self.ysem, self.zsem = scratch
        self.owners, self.nz = part.shape[:2]
        slab = lax.axis_index("slab")
        self.z, self.y = slab // Y, mod(slab, Y)

    def _owns(self, y):
        return True if self.owners == Y else y < self.owners

    def _y(self, d, give):
        y, to = self.y, mod(self.y + d, Y)
        src = self.out.at[y] if give else self.part.at[to]
        dst = self.out.at[y] if give else self.from_y.at[y]
        return remote(src, dst, self.ysem.at[give, 0, to], self.ysem.at[give, 1, y], slab=self.z * Y + to)

    def _y_in(self, d, give):
        of = mod(self.y + d, Y)
        dst = self.out.at[of] if give else self.from_y.at[of]
        return remote(dst, dst, self.ysem.at[give, 0, of], self.ysem.at[give, 1, of], slab=self.z * Y + of)

    def _z(self, d, give):
        z, to = self.z, mod(self.z + d, self.nz)
        src = self.out.at[self.y, z] if give else self.sum_y.at[to]
        dst = self.out.at[self.y, z] if give else self.from_z.at[z]
        return remote(src, dst, self.zsem.at[give, 0, to], self.zsem.at[give, 1, z], slab=to * Y + self.y)

    def _z_in(self, d, give):
        of = mod(self.z + d, self.nz)
        dst = self.out.at[self.y, of] if give else self.from_z.at[of]
        return remote(dst, dst, self.zsem.at[give, 0, of], self.zsem.at[give, 1, of], slab=of * Y + self.y)

    def _each_z(self, step):
        def body(d, carry):
            step(d)
            return carry

        lax.fori_loop(1, self.nz, body, 0)

    def start(self):
        for d in range(1, Y):
            when(self._owns(mod(self.y + d, Y)), lambda: self._y(d, 0).start())

    def along_z(self):
        def step():
            for d in range(1, Y):
                self._y_in(d, 0).wait_recv()
            total = self.part[self.y].astype(jnp.float32)
            for d in range(1, Y):
                total = total + self.from_y[mod(self.y + d, Y)].astype(jnp.float32)
            self.sum_y[...] = total.astype(self.sum_y.dtype)
            self._each_z(lambda d: self._z(d, 0).start())

        when(self._owns(self.y), step)

    def hand_out_z(self, finish):
        def step():
            self._each_z(lambda d: self._z_in(d, 0).wait_recv())
            total = self.sum_y[self.z].astype(jnp.float32)
            for d in range(1, self.nz):
                total = total + self.from_z[mod(self.z + d, self.nz)].astype(jnp.float32)
            self.out[self.y, self.z] = finish(total).astype(self.out.dtype)
            self._each_z(lambda d: self._z(d, 1).start())

        when(self._owns(self.y), step)

    def hand_out_y(self):
        def step():
            self._each_z(lambda d: self._z_in(d, 1).wait_recv())
            for d in range(1, Y):
                self._y(d, 1).start()

        when(self._owns(self.y), step)

    def end(self):
        for d in range(1, Y):
            when(self._owns(mod(self.y + d, Y)), lambda: self._y_in(d, 1).wait_recv())

    def settle(self):
        for d in range(1, Y):
            when(self._owns(mod(self.y + d, Y)), lambda: self._y(d, 0).wait_send())

        def mine():
            for d in range(1, Y):
                self._y(d, 1).wait_send()

            def done(d):
                self._z(d, 0).wait_send()
                self._z(d, 1).wait_send()

            self._each_z(done)

        when(self._owns(self.y), mine)


class TorusGather:
    @staticmethod
    def scratch(nz):
        return [
            DMA((2, nz, 2)), DMA((nz, 2)), DMA((3,)), DMA((3,)),
            DMA((2, nz)), DMA((nz,)), DMA((2, nz)), DMA((2, nz)), DMA((nz,)), DMA((nz,)), DMA((3,)),
            DMA((2, 2)), DMA((2, 2)), DMA((2,)), DMA((2,)),
        ]

    def __init__(self, wa, wb, ga, gb, sems):
        self.wa, self.wb, self.ga, self.gb = wa, wb, ga, gb
        (self.az_s, self.az_r, self.ay_s, self.ay_r, self.bz_s, self.bz_r,
         self.by_s, self.by_r, self.bo_s, self.bo_r, self.own_sem,
         self.ly_s, self.ly_r, self.lo_s, self.lo_r) = sems
        self.nz = nz = gb.shape[0]
        self.half = nz // 2
        slab = lax.axis_index("slab")
        self.z, self.y = z, y = slab // Y, mod(slab, Y)
        self.next = mod(z + 1, nz), mod(z + nz - 1, nz)
        self.right, self.left, self.across = mod(y + 1, Y), mod(y + Y - 1, Y), mod(y + 2, Y)
        self.sides = self.right, self.left
        self.parts = (pl.ds(0, self.half), pl.ds(self.half, self.half))
        self.sent = []

    def _go(self, copy):
        copy.start()
        self.sent.append(copy)

    def _landed(self, dst, sem):
        remote(dst, dst, self.own_sem.at[2], sem, slab=self.z * Y + self.right).wait_recv()

    def _pair(self, origin, p):
        return self.ga.at[origin, pl.ds(2 * p, 2)]

    def _a_z(self, origin, p, way):
        block = self._pair(origin, p)
        self._go(remote(block, block, self.az_s.at[way, origin, p], self.az_r.at[origin, p],
                        slab=self.next[way] * Y + self.y))

    def _b_z(self, origin, src, way):
        self._go(remote(src, self.gb.at[origin, self.y], self.bz_s.at[way, origin], self.bz_r.at[origin],
                        slab=self.next[way] * Y + self.y))

    def _two(self, origin, j):
        return self.gb.at[origin, j, pl.ds(0, 2)]

    def _b_y(self, origin, src):
        for way, to in enumerate(self.sides):
            self._go(remote(src, self._two(origin, self.y), self.by_s.at[way, origin], self.by_r.at[way, origin],
                            slab=self.z * Y + to))

    def _b_relay(self, origin):
        self._landed(self._two(origin, self.left), self.by_r.at[0, origin])
        self._landed(self._two(origin, self.right), self.by_r.at[1, origin])
        turn = 1 - 2 * mod(origin, 2)
        block = self._two(origin, mod(self.y - turn + Y, Y))
        self._go(remote(block, block, self.bo_s.at[origin], self.bo_r.at[origin],
                        slab=self.z * Y + mod(self.y + turn + Y, Y)))

    def start(self, meanwhile):
        z, y, wa, wb = self.z, self.y, self.wa, self.wb
        self._b_z(z, wb, 0)
        self._b_z(z, wb, 1)
        for i, to in enumerate((self.right, self.left, self.across)):
            self._go(remote(wa, self.ga.at[z, y], self.ay_s.at[i], self.ay_r.at[i], slab=z * Y + to))
        self.own_a = pltpu.make_async_copy(wa, self.ga.at[z, y], self.own_sem.at[0])
        self.own_a.start()
        self._b_y(z, wb.at[pl.ds(0, 2)])
        self.own_b = pltpu.make_async_copy(wb, self.gb.at[z, y], self.own_sem.at[1])
        self.own_b.start()
        meanwhile()
        odd = mod(y, 2)
        self._landed(self.ga.at[z, y + 1 - 2 * odd], self.ay_r.at[1 - odd])
        self.own_a.wait()
        self._a_z(z, y // 2, 0)
        self._a_z(z, y // 2, 1)
        self._landed(self.ga.at[z, mod(y + Y - 1 + 2 * odd, Y)], self.ay_r.at[odd])
        self._landed(self.ga.at[z, self.across], self.ay_r.at[2])
        self._a_z(z, 1 - y // 2, 0)
        self._a_z(z, 1 - y // 2, 1)

    def step(self, t):
        nz, half, y = self.nz, self.half, self.y
        ways = [(mod(self.z - t + nz, nz), 0, half)]
        if t < half:
            ways.append((mod(self.z + t, nz), 1, half - 1))
        for origin, way, last in ways:
            block = self.gb.at[origin, y]
            self._landed(block, self.bz_r.at[origin])
            if t < last:
                self._b_z(origin, block, way)
            two = self._two(origin, y)
            self._b_y(origin, two)
            if t == half:
                self._go(remote(two, two, self.bo_s.at[origin], self.bo_r.at[origin],
                                slab=self.z * Y + self.across))
        for p in (y // 2, 1 - y // 2):
            for origin, way, last in ways:
                self._landed(self._pair(origin, p), self.az_r.at[origin, p])
                if t < last:
                    self._a_z(origin, p, way)
        self._b_relay(mod(self.z - t + 1 + nz, nz))
        if t > 1:
            self._b_relay(mod(self.z + t - 1, nz))

    def across_landed(self, t):
        origins = [mod(self.z - t + self.nz, self.nz)]
        if 0 < t < self.half:
            origins.append(mod(self.z + t, self.nz))
        for origin in origins:
            if t == self.half:
                self._landed(self._two(origin, self.left), self.by_r.at[0, origin])
                self._landed(self._two(origin, self.right), self.by_r.at[1, origin])
            self._landed(self._two(origin, self.across), self.bo_r.at[origin])

    def _late(self, part, j):
        return self.gb.at[self.parts[part], j, 2]

    def late_start(self):
        for turn in range(2):
            for way in range(2):
                part = way if turn == 0 else 1 - way
                block = self._late(part, self.y)
                self._go(remote(block, block, self.ly_s.at[way, part], self.ly_r.at[way, part],
                                slab=self.z * Y + self.sides[way]))

    def late_relay(self):
        for way in range(2):
            block = self._late(way, self.sides[1 - way])
            self._landed(block, self.ly_r.at[way, way])
            self._go(remote(block, block, self.lo_s.at[way], self.lo_r.at[way], slab=self.z * Y + self.sides[way]))

    def late_end(self):
        for way in range(2):
            self._landed(self._late(1 - way, self.sides[1 - way]), self.ly_r.at[way, 1 - way])
        for way in range(2):
            self._landed(self._late(way, self.across), self.lo_r.at[way])

    def settle(self):
        for copy in self.sent:
            copy.wait_send()


def row_scale(values):
    return lax.rsqrt(jnp.mean(values * values, axis=-1, keepdims=True) + norm_eps)


OPERANDS = 15
FETCH_ORDER = (2, 3, 4, 5, 0, 1, 6, 7, 8, 9, 10, 11, 12, 13, 14)
QKV_SEMS = 15


def whole_kernel(*refs):
    f32, bf16 = jnp.float32, jnp.bfloat16

    def take(count):
        nonlocal refs
        some, refs = refs[:count], refs[count:]
        return some

    fetched = take(OPERANDS)
    out, text_final = take(2)
    held = take(OPERANDS)
    video, text, wq, wk, wv, wo, twq, twk, twv, qg, kg, tqg, tkg, mask, window = held
    (fetch_sem, wb, ga, gb, normed, tnormed, tweight, text_part, text_rows, acc) = take(10)
    (q, k, v, num, den, num_out, num_in, den_in, attn, live, tsum_part, text_out) = take(12)
    (part, pair, far, near) = take(4)
    qkv = TorusGather(wq, wb, ga, gb, take(QKV_SEMS))
    text_sum = SlabSum(text_part, text_rows, take(5))
    attn_sum = SlabSum(tsum_part, text_out, take(5))
    q_s, q_r, k_s, k_r, v_s, v_r, n_s, n_r, d_s, d_r = take(10)
    pair_s, pair_r, far_s, far_r, near_s, near_r = take(6)

    nz = gb.shape[0]
    nx = part.shape[0]
    slab, head = lax.axis_index("slab"), lax.axis_index("head")
    slab_count = lax.axis_size("slab")
    z, y = slab // Y, mod(slab, Y)
    row, column = slab // COLUMN_TILES, mod(slab, COLUMN_TILES)
    above, below = mod(slab + slab_count - COLUMN_TILES, slab_count), mod(slab + COLUMN_TILES, slab_count)
    has_left, has_right = column > 0, column < COLUMN_TILES - 1
    has_above, has_below = row > 0, row < slab_count // COLUMN_TILES - 1
    jump_left, jump_right = has_left & (y == 0), has_right & (y == Y - 1)
    x, core = head // 2, mod(head, 2)
    x_right, x_left, x_far = mod(x + 1, nx), mod(x + nx - 1, nx), mod(x + 2, nx)
    other, right, left = x * 2 + 1 - core, x_right * 2 + core, x_left * 2 + core
    depth, width = wq.shape
    heads = width // HEAD_SIZE
    tokens, model = video.shape
    txt = text.shape[0]
    score_scale = 1.0 / math.sqrt(HEAD_SIZE)
    steps = nz // 2
    nt = (((1,), (1,)), ((), ()))

    fetches = [
        pltpu.make_async_copy(src, dst, fetch_sem.at[i]) for i, (src, dst) in enumerate(zip(fetched, held))
    ]
    for i in FETCH_ORDER:
        fetches[i].start()

    barrier, peers = hello_slab(z, y, nz)
    greet((), (other, right, left))

    @pl.when(jump_left)
    def _():
        greet((slab - 1,))

    @pl.when(jump_right)
    def _():
        greet((slab + 1,))

    for i in FETCH_ORDER[:4]:
        fetches[i].wait()
    for i, weight in enumerate((wk, wv, wo)):
        wb[i] = weight[...]
    pl.semaphore_wait(barrier, peers + 3 + jump_left.astype(jnp.int32) + jump_right.astype(jnp.int32))
    def normalize_video(i, carry):
        at = pl.ds(pl.multiple_of(i * 16, 16), 16)
        values = video[at, :].astype(f32)
        center = values - jnp.mean(values, axis=-1, keepdims=True)
        normed[at, :] = (center * row_scale(center)).astype(bf16)
        return carry

    blocks = tokens // 16
    early = blocks // 4

    def first_rows():
        fetches[0].wait()
        lax.fori_loop(0, early, normalize_video, 0)

    qkv.start(first_rows)

    span = tweight.shape[0]
    aligned = jnp.minimum(slab * depth // LANES * LANES, model - span)
    aligned = pl.multiple_of(aligned, LANES)
    offset = pl.multiple_of(slab * depth - aligned, 16)
    share = nz // heads

    def fill_text_weights():
        tweight[...] = jnp.zeros_like(tweight)
        for i, weight in enumerate((twq, twk, twv)):
            tweight[pl.ds(offset, depth), i * width : (i + 1) * width] = weight[...]

    def normalize_text(i, carry):
        at = pl.ds(pl.multiple_of(i * 16, 16), 16)
        values = text[at, :].astype(f32)
        mean = jnp.mean(values, axis=-1, keepdims=True)
        scale = row_scale(values - mean)
        columns = text[at, pl.ds(aligned, span)].astype(f32)
        tnormed[at, :] = ((columns - mean) * scale).astype(bf16)
        return carry

    def multiply_text():
        for i in range(3):
            product = jnp.dot(
                tnormed[...], tweight[:, i * width : (i + 1) * width], preferred_element_type=f32
            ).astype(bf16)
            for h in range(heads):
                block = product[:, h * HEAD_SIZE : (h + 1) * HEAD_SIZE]
                text_part[i, h * share : (h + 1) * share] = block.reshape(share, txt // share, HEAD_SIZE)

    def finish_text(total):
        gain = jnp.where(y == 0, tqg[...], tkg[...])
        return jnp.where(y == 2, total, total * row_scale(total) * gain)

    for t in range(1, steps + 1):
        qkv.step(t)
        if t == 1:
            for i in FETCH_ORDER[5:]:
                fetches[i].wait()
            fill_text_weights()
            lax.fori_loop(0, txt // 32, normalize_text, 0)
        if t == 2:
            lax.fori_loop(txt // 32, txt // 16, normalize_text, 0)
            multiply_text()
            text_sum.start()
        if t == 4:
            text_sum.along_z()
        if t == 7:
            text_sum.hand_out_z(finish_text)
        rest = blocks - early
        lax.fori_loop(early + (t - 1) * rest // steps, early + t * rest // steps, normalize_video, 0)

    qkv.own_b.wait()
    qkv.late_start()

    acc[...] = jnp.zeros_like(acc)
    group = 4 if nz % 4 == 0 else nz
    span = group * Y * depth

    def multiply_query(c, carry):
        rows = normed[:, pl.ds(pl.multiple_of(c * span, span), span)]
        acc[:, :width] += jnp.dot(
            rows, ga[pl.ds(c * group, group)].reshape(span, width), preferred_element_type=f32
        )
        return carry

    lax.fori_loop(0, nz // group, multiply_query, 0)
    rows_out = []
    for h in range(heads):
        values = acc[:, h * HEAD_SIZE : (h + 1) * HEAD_SIZE]
        q[0, h] = (values * row_scale(values) * qg[...]).astype(bf16)
        to_below = remote(q.at[0, h], q.at[1, h], q_s.at[0, h], q_r.at[0, h], slab=below)
        to_above = remote(q.at[0, h], q.at[2, h], q_s.at[1, h], q_r.at[1, h], slab=above)
        to_below.start()
        to_above.start()
        rows_out.append((to_below, to_above))
    text_sum.hand_out_y()

    pair_depth = 2 * Y * depth

    def multiply_rest(i, carry):
        at = mod(z // 2 + i + nz // 2 - 2, nz // 2)
        rows = normed[:, pl.ds(pl.multiple_of(at * pair_depth, pair_depth), pair_depth)]
        for j in range(2):
            acc[:, (j + 1) * width : (j + 2) * width] += jnp.dot(
                rows, gb[pl.ds(at * 2, 2), :, j].reshape(pair_depth, width), preferred_element_type=f32
            )
        return carry

    near_steps = 5
    for t in range(near_steps + 1):
        qkv.across_landed(t)
    lax.fori_loop(0, 5, multiply_rest, 0)
    for t in range(near_steps + 1, steps + 1):
        qkv.across_landed(t)
    lax.fori_loop(5, nz // 2, multiply_rest, 0)

    to_right, to_left = [], []
    for h in range(heads):
        values = acc[:, width + h * HEAD_SIZE : width + (h + 1) * HEAD_SIZE]
        k[0, h] = (values * row_scale(values) * kg[...]).astype(bf16)
        v[0, h] = acc[:, 2 * width + h * HEAD_SIZE : 2 * width + (h + 1) * HEAD_SIZE].T.astype(bf16)
        right_now = [
            remote(k.at[0, h], k.at[1, h], k_s.at[0, h], k_r.at[0, h], slab=slab + 1),
            remote(v.at[0, h], v.at[1, h], v_s.at[0, h], v_r.at[0, h], slab=slab + 1),
        ]
        left_now = [
            remote(k.at[0, h], k.at[2, h], k_s.at[1, h], k_r.at[1, h], slab=slab - 1),
            remote(v.at[0, h], v.at[2, h], v_s.at[1, h], v_r.at[1, h], slab=slab - 1),
        ]
        to_right += right_now
        to_left += left_now

        def start_all(copies):
            for copy in copies:
                copy.start()

        pl.when(has_right)(functools.partial(start_all, right_now))
        pl.when(has_left)(functools.partial(start_all, left_now))

    @pl.when(jnp.logical_not(has_left))
    def _():
        k[1] = jnp.zeros_like(k[1])
        v[1] = jnp.zeros_like(v[1])

    @pl.when(jnp.logical_not(has_right))
    def _():
        k[2] = jnp.zeros_like(k[2])
        v[2] = jnp.zeros_like(v[2])

    def scores(keys, queries):
        return jnp.exp(lax.dot_general(keys, queries, nt, preferred_element_type=f32) * score_scale)

    def weigh(values, e):
        return jnp.dot(values, e.astype(bf16), preferred_element_type=f32)

    def column_sum(e):
        return jnp.sum(e, axis=0, keepdims=True)

    tsum_part[heads] = jnp.zeros_like(tsum_part[heads])
    for h in range(heads):
        e = scores(k[0, h], q[0, h])
        num[0, h] = weigh(v[0, h], e)
        den[0, h, 0:1] = column_sum(e)

    qkv.late_relay()

    for h in range(heads):
        for copy in rows_out[h]:
            copy.wait_recv()

        def neighbour(tile, carry, h=h):
            e = scores(k[0, h], q[tile, h])
            num[tile, h] = weigh(v[0, h], e)
            den[tile, h] = jnp.broadcast_to(column_sum(e), den.shape[2:])
            return carry

        lax.fori_loop(1, 3, neighbour, 0)
    live[...] = jnp.broadcast_to(mask[...].astype(f32), live.shape).T
    is_first = jnp.where(slab == 0, 1.0, 0.0)
    text_sum.end()

    def text_head(i, h):
        return text_rows[i, h * share : (h + 1) * share].reshape(txt, HEAD_SIZE)

    text_values = []
    for h in range(heads):
        tq = text_head(0, h)
        text_values.append(text_head(2, h).astype(f32).T.astype(bf16))
        e = scores(k[0, h], tq)
        own = scores(text_head(1, h), tq) * live[...] * is_first
        total = weigh(v[0, h], e) + weigh(text_values[h], own)
        tsum_part[h] = total.reshape(tsum_part.shape[1:])
        tsum_part[heads, 0, h : h + 1] = column_sum(e) + column_sum(own)
    attn_sum.start()

    live_wide = jnp.concatenate([live[...]] * (tokens // txt), axis=1)
    for h in range(heads):
        e = scores(text_head(1, h), q[0, h]) * live_wide
        num[0, h] += weigh(text_values[h], e)
        den[0, h, 0:1] += column_sum(e)

    text_sum.settle()
    attn_sum.along_z()

    def add_side(slot, tile, h):
        reach = jnp.where(jnp.where(slot == 1, has_left, has_right), 1.0, 0.0)
        e = scores(k[slot, h], q[tile, h])
        e = e * (reach * window[1, head * heads + h].astype(f32))
        num[tile, h] += weigh(v[slot, h], e)
        den[tile, h, 0:1] += column_sum(e)

    back = []
    for h in range(heads):

        @pl.when(has_left)
        def _():
            for sem, dst in ((k_r, k), (v_r, v)):
                remote(dst.at[1, h], dst.at[1, h], sem.at[0, h], sem.at[0, h], slab=slab - 1).wait_recv()

        @pl.when(has_right)
        def _():
            for sem, dst in ((k_r, k), (v_r, v)):
                remote(dst.at[2, h], dst.at[2, h], sem.at[1, h], sem.at[1, h], slab=slab + 1).wait_recv()

        def side(i, carry, h=h):
            add_side(1 + i % 2, 1 + i // 2, h)
            return carry

        lax.fori_loop(0, 4, side, 0)
        for tile in (1, 2):
            num_out[tile - 1, h] = num[tile, h].astype(bf16)
        now = [
            remote(num_out.at[0, h], num_in.at[1, h], n_s.at[1, h], n_r.at[1, h], slab=above),
            remote(num_out.at[1, h], num_in.at[0, h], n_s.at[0, h], n_r.at[0, h], slab=below),
            remote(den.at[1, h], den_in.at[1, h], d_s.at[1, h], d_r.at[1, h], slab=above),
            remote(den.at[2, h], den_in.at[0, h], d_s.at[0, h], d_r.at[0, h], slab=below),
        ]
        for copy in now:
            copy.start()
        back.append(now)

    def own_side(i, carry):
        add_side(1 + i % 2, 0, i // 2)
        return carry

    lax.fori_loop(0, 2 * heads, own_side, 0)
    attn_sum.hand_out_z(lambda total: total)
    for h in range(heads):
        for copy in back[h]:
            copy.wait_recv()
        total, under = num[0, h], den[0, h, 0:1]
        for side_row, exists in ((0, has_above), (1, has_below)):
            reach = jnp.where(exists, 1.0, 0.0) * window[0, head * heads + h].astype(f32)
            total = total + num_in[side_row, h].astype(f32) * reach
            under = under + den_in[side_row, h, 0:1] * reach
        attn[:, h * HEAD_SIZE : (h + 1) * HEAD_SIZE] = (total / under).T.astype(bf16)

    qkv.late_end()
    order = (x_far, x_right, x_left, x)
    rows = tokens // nx
    halves = part.shape[2]
    pairs = []

    def send_pair(xx):
        mine = attn[pl.ds(pl.multiple_of(xx * rows, 16), rows), :]
        for half in range(halves):
            weight = gb[half * nz // halves : (half + 1) * nz // halves, :, 2].reshape(model // halves, width)
            product = lax.dot_general(mine, weight, nt, preferred_element_type=f32).astype(bf16)
            for c in range(2):
                part[xx, c, half] = product[c * rows // 2 : (c + 1) * rows // 2]
        pairs.append(remote(part.at[xx, 1 - core], pair.at[xx], pair_s.at[xx], pair_r.at[xx], head=other))
        pairs[-1].start()

    def pair_sum(xx):
        remote(pair.at[xx], pair.at[xx], pair_s.at[xx], pair_r.at[xx], head=other).wait_recv()
        pair[xx] = (pair[xx].astype(f32) + part[xx, core].astype(f32)).astype(bf16)

    send_pair(x_far)
    send_pair(x_right)
    send_pair(x_left)
    pair_sum(x_far)
    fars = [
        remote(pair.at[x_far, 0], far.at[0], far_s.at[0], far_r.at[0], head=right),
        remote(pair.at[x_far, 1], far.at[1], far_s.at[1], far_r.at[1], head=left),
    ]
    for copy in fars:
        copy.start()
    pair_sum(x_right)
    pair_sum(x_left)
    nears = [
        remote(pair.at[x_right, 1], near.at[0, 1], near_s.at[0, 1], near_r.at[0, 1], head=right),
        remote(pair.at[x_left, 0], near.at[1, 0], near_s.at[1, 0], near_r.at[1, 0], head=left),
        remote(pair.at[x_right, 0], near.at[0, 0], near_s.at[0, 0], near_r.at[0, 0], head=right),
        remote(pair.at[x_left, 1], near.at[1, 1], near_s.at[1, 1], near_r.at[1, 1], head=left),
    ]
    nears[0].start()
    nears[1].start()
    send_pair(x)
    attn_sum.hand_out_y()
    pair_sum(x)
    fars[0].wait_recv()
    pair[x_right, 0] = (pair[x_right, 0].astype(f32) + far[0].astype(f32)).astype(bf16)
    nears[2].start()
    fars[1].wait_recv()
    pair[x_left, 1] = (pair[x_left, 1].astype(f32) + far[1].astype(f32)).astype(bf16)
    nears[3].start()
    qkv.settle()
    for copy in (*sum(rows_out, ()), *sum(back, []), *pairs):
        copy.wait_send()

    @pl.when(has_right)
    def _():
        for copy in to_right:
            copy.wait_send()

    @pl.when(has_left)
    def _():
        for copy in to_left:
            copy.wait_send()

    for copy in nears:
        copy.wait_recv()
    for half in range(halves):
        at = half * model // halves
        out[:, at : at + model // halves] = (
            pair[x, half].astype(f32) + near[0, half].astype(f32) + near[1, half].astype(f32)
        ).astype(bf16)

    attn_sum.end()
    for h in range(heads):
        total = text_out[h].reshape(HEAD_SIZE, txt) / text_out[heads, 0, h : h + 1]
        text_final[:, h * HEAD_SIZE : (h + 1) * HEAD_SIZE] = total.T.astype(bf16)
    attn_sum.settle()
    for copy in (*fars, *nears):
        copy.wait_send()


def run_whole(slab_count, head_count, operands):
    video, text, wq = operands[0], operands[1], operands[2]
    depth, width = wq.shape
    tokens, model = video.shape
    txt = text.shape[0]
    heads = width // HEAD_SIZE
    nz, nx = slab_count // Y, head_count // 2
    rows = tokens // head_count
    bf16, f32 = jnp.bfloat16, jnp.float32
    text_block = jax.ShapeDtypeStruct((3, nz, txt * heads // nz, HEAD_SIZE), bf16)
    sum_block = jax.ShapeDtypeStruct((heads + 1, nz, HEAD_SIZE // nz, txt), f32)
    half = model // 2
    vmem = pl.BlockSpec(memory_space=VMEM)
    return pl.pallas_call(
        whole_kernel,
        out_shape=(
            jax.ShapeDtypeStruct((rows, model), bf16),
            jax.ShapeDtypeStruct((txt, width), bf16),
        ),
        in_specs=[pl.BlockSpec(memory_space=pltpu.HBM)] * OPERANDS,
        out_specs=(vmem, vmem),
        scratch_shapes=[
            *(VMEM(a.shape, a.dtype) for a in operands[:-1]),
            pltpu.SMEM(operands[-1].shape, operands[-1].dtype),
            DMA((OPERANDS,)),
            VMEM((3, depth, width), bf16),
            VMEM((nz, Y, depth, width), bf16),
            VMEM((nz, Y, 3, depth, width), bf16),
            VMEM((tokens, model), bf16),
            VMEM((txt, 2 * LANES), bf16),
            VMEM((2 * LANES, 3 * width), bf16),
            VMEM(text_block.shape, bf16),
            VMEM(text_block.shape, bf16),
            VMEM((tokens, 3 * width), f32),
            VMEM((3, heads, tokens, HEAD_SIZE), bf16),
            VMEM((3, heads, tokens, HEAD_SIZE), bf16),
            VMEM((3, heads, HEAD_SIZE, tokens), bf16),
            VMEM((3, heads, HEAD_SIZE, tokens), f32),
            VMEM((3, heads, 8, tokens), f32),
            VMEM((2, heads, HEAD_SIZE, tokens), bf16),
            VMEM((2, heads, HEAD_SIZE, tokens), bf16),
            VMEM((2, heads, 8, tokens), f32),
            VMEM((tokens, width), bf16),
            VMEM((txt, txt), f32),
            VMEM(sum_block.shape, f32),
            VMEM(sum_block.shape, f32),
            VMEM((nx, 2, 2, rows, half), bf16),
            VMEM((nx, 2, rows, half), bf16),
            VMEM((2, rows, half), bf16),
            VMEM((2, 2, rows, half), bf16),
            *TorusGather.scratch(nz),
            *SlabSum.scratch(text_block),
            *SlabSum.scratch(sum_block),
            *[DMA((2, heads))] * 10,
            DMA((nx,)), DMA((nx,)), DMA((2,)), DMA((2,)), DMA((2, 2)), DMA((2, 2)),
        ],
        compiler_params=pltpu.CompilerParams(
            collective_id=0, has_side_effects=True, vmem_limit_bytes=32 * MIB
        ),
        name="whole",
    )(*(pltpu.with_memory_space_constraint(a, pltpu.HBM) for a in operands))


def on_device(
    video_token_state,
    text_tokens,
    text_mask,
    head_window,
    video_query_weight,
    video_key_weight,
    video_value_weight,
    wout_video,
    wquery_text,
    wkey_text,
    wvalue_text,
    video_query_gain,
    video_key_gain,
    qgain_text,
    kgain_text,
):
    operands = (
        video_token_state, text_tokens,
        video_query_weight, video_key_weight, video_value_weight, wout_video.T,
        wquery_text, wkey_text, wvalue_text,
        *(row.reshape(1, -1) for row in (video_query_gain, video_key_gain, qgain_text, kgain_text, text_mask)),
        head_window.T,
    )
    return run_whole(lax.axis_size("slab"), lax.axis_size("head"), operands)


def solution(mesh):
    return jax.shard_map(
        on_device,
        mesh=mesh,
        in_specs=(
            P("slab", None),
            P(),
            P(),
            P(),
            P("slab", "head"),
            P("slab", "head"),
            P("slab", "head"),
            P("head", "slab"),
            P("slab", "head"),
            P("slab", "head"),
            P("slab", "head"),
            P(),
            P(),
            P(),
            P(),
        ),
        out_specs=(P(("slab", "head"), None), P(None, "head")),
        check_vma=False,
    )
```

time: 1330 us -> 117 us (0.09)
  waiting for transfers between devices: 1100 us -> 0 us
  blocking collectives: 141 us -> 0 us
  Pallas kernels: 0 us -> 113 us
  matrix products: 26.5 us -> 0 us
  starting transfers between devices: 22.6 us -> 0 us
  between operations: 14.3 us -> 0.64 us
    all_gather x7 -> x0, waiting for transfers between devices: 907 us -> none  [the longest x1 136 us: on_device(): lax.all_gather(video_value_weight, 'slab', axis=0, tiled=True)]
    psum x1 -> x0, blocking collectives: 141 us -> none  [on_device(): lax.psum((far_numerator, far_denominator), 'slab')]
    psum x1 -> x0, waiting for transfers between devices: 115 us -> none  [on_device(): lax.psum((far_numerator, far_denominator), 'slab')]
    pallas_call x0 -> x1, Pallas kernels: none -> 113 us  [run_whole(): pl.pallas_call(whole_kernel, out_shape=(jax.ShapeDtypeStruct((rows, model...]
    ppermute x8 -> x0, waiting for transfers between devices: 38.4 us -> none  [from_behind(): return lax.ppermute(array, axis, pairs)]
    reduce_scatter x1 -> x0, waiting for transfers between devices: 34.5 us -> none  [on_device(): lax.psum_scatter(jnp.dot(video_attn, out_weights, preferred_element_type=...]
    dot_general x15 -> x0, matrix products: 26.5 us -> none  [the longest x6 15.7 us: merge_into(): result.append(jnp.dot(source, segment, preferred_element_type=jnp.float32))]
    ppermute x8 -> x0, starting transfers between devices: 22.3 us -> none  [from_behind(): return lax.ppermute(array, axis, pairs)]
  transfers between devices with their start and end apart: 17 -> 0, of which waited for: 12 -> 0; matrix products, arithmetic and copies ran while one was open for 4% -> 0% of each run, Pallas kernels for 0% -> 0%
where the time goes in v1:
time: 117 us; the launch traced here: 115 us
  Pallas kernels  113 us (97%)
  local copies, waits for them, and re-layouts  1.35 us (1%)
    pallas_call x1, Pallas kernels, run_whole(): pl.pallas_call(whole_kernel, out_shape=(jax.ShapeDtypeStruct((rows, model...  113 us

profile of v1, /device:TPU:6, one launch (start us, length us, event | category | flops | bytes accessed | tf_op | source)
XLA Modules:
  0.0 115.2 jit_solution(15674417722175461312)
XLA Ops:
  0.6 113.3 %whole.1 = (bf16[48,3072]{1,0:T(8,128)(2,1)S(1)}, bf16[128,256]{1,0:T(8,128)(2,1)S(1)}) custom-call(bf16[384,3072]{1,0:T(8,128)(2,1)} %refs_0_.1, bf16[128,3072]{1,0:T(8,128)(2,1)} %refs_1_.1, bf16[48,256]{1,0:T(8,128)(2,1)} %refs_2_.1, bf16[48,256]{1,0:T(8,128)(2,1)} %refs_3_.1, bf16[48,256]{1,0:T(8,128)(2,1)} %refs_4_.1, bf16[48,256]{1,0:T(8,128)(2,1)} %bitcast.7, ...), custom_call_target="tpu_custom_call" | custom-call | tf_op jit(solution)/shard_map/whole/pallas_call | solution.py:736
  113.9 0.7 copy.19
  114.6 0.6 copy.20

commit v2 on v1

--- a/solution.py
+++ b/solution.py
@@ -11,6 +11,7 @@
 HEAD_SIZE = 128
 COLUMN_TILES = 8
 Y = 4
+NB = 4
 MIB = 1 << 20
 LANES = 128
 VMEM = pltpu.VMEM
@@ -39,14 +40,6 @@
     return barrier
 
 
-def when(condition, step):
-    if isinstance(condition, bool):
-        if condition:
-            step()
-    else:
-        pl.when(condition)(step)
-
-
 def hello_slab(z, y, nz):
     barrier = pltpu.get_barrier_semaphore()
 
@@ -67,24 +60,31 @@
 class SlabSum:
     @staticmethod
     def scratch(block):
-        owners, nz, rows, lanes = block.shape
+        owners, na, nb, rows, lanes = block.shape
         return [
-            VMEM((Y, nz, rows, lanes), block.dtype),
-            VMEM((nz, rows, lanes), block.dtype),
-            VMEM((nz, rows, lanes), block.dtype),
+            VMEM((Y, na, nb, rows, lanes), block.dtype),
+            VMEM((na, nb, rows, lanes), block.dtype),
+            VMEM((nb, na, rows, lanes), block.dtype),
+            VMEM((na, rows, lanes), block.dtype),
+            VMEM((na, rows, lanes), block.dtype),
             DMA((2, 2, Y)),
-            DMA((2, 2, nz)),
+            DMA((2, 2, nb)),
+            DMA((2, 2, na)),
         ]
 
     def __init__(self, part, out, scratch):
         self.part, self.out = part, out
-        self.from_y, self.sum_y, self.from_z, self.ysem, self.zsem = scratch
-        self.owners, self.nz = part.shape[:2]
+        (self.from_y, self.sum_y, self.from_b, self.sum_b, self.from_a, self.ysem, self.bsem, self.asem) = scratch
+        self.owners, self.na, self.nb = part.shape[:3]
         slab = lax.axis_index("slab")
         self.z, self.y = slab // Y, mod(slab, Y)
+        self.a, self.b = self.z // self.nb, mod(self.z, self.nb)
 
     def _owns(self, y):
-        return True if self.owners == Y else y < self.owners
+        return y < self.owners
+
+    def _slab(self, a, b, y):
+        return (a * self.nb + b) * Y + y
 
     def _y(self, d, give):
         y, to = self.y, mod(self.y + d, Y)
@@ -97,86 +97,106 @@
         dst = self.out.at[of] if give else self.from_y.at[of]
         return remote(dst, dst, self.ysem.at[give, 0, of], self.ysem.at[give, 1, of], slab=self.z * Y + of)
 
-    def _z(self, d, give):
-        z, to = self.z, mod(self.z + d, self.nz)
-        src = self.out.at[self.y, z] if give else self.sum_y.at[to]
-        dst = self.out.at[self.y, z] if give else self.from_z.at[z]
-        return remote(src, dst, self.zsem.at[give, 0, to], self.zsem.at[give, 1, z], slab=to * Y + self.y)
-
-    def _z_in(self, d, give):
-        of = mod(self.z + d, self.nz)
-        dst = self.out.at[self.y, of] if give else self.from_z.at[of]
-        return remote(dst, dst, self.zsem.at[give, 0, of], self.zsem.at[give, 1, of], slab=of * Y + self.y)
-
-    def _each_z(self, step):
-        def body(d, carry):
-            step(d)
-            return carry
-
-        lax.fori_loop(1, self.nz, body, 0)
+    def _b(self, d, give, coming=False):
+        b, other = self.b, mod(self.b + d, self.nb)
+        sent, kept = (other, b) if coming else (b, other)
+        src = self.out.at[self.y, :, sent] if give else self.sum_y.at[:, kept]
+        dst = self.out.at[self.y, :, sent] if give else self.from_b.at[sent]
+        if coming:
+            src = dst
+        return remote(src, dst, self.bsem.at[give, 0, other], self.bsem.at[give, 1, sent],
+                      slab=self._slab(self.a, other, self.y))
+
+    def _a(self, d, give, coming=False):
+        a, other = self.a, mod(self.a + d, self.na)
+        sent = other if coming else a
+        src = self.out.at[self.y, sent, self.b] if give else self.sum_b.at[other]
+        dst = self.out.at[self.y, sent, self.b] if give else self.from_a.at[sent]
+        if coming:
+            src = dst
+        return remote(src, dst, self.asem.at[give, 0, other], self.asem.at[give, 1, sent],
+                      slab=self._slab(other, self.b, self.y))
 
     def start(self):
         for d in range(1, Y):
-            when(self._owns(mod(self.y + d, Y)), lambda: self._y(d, 0).start())
-
-    def along_z(self):
-        def step():
+            pl.when(self._owns(mod(self.y + d, Y)))(lambda d=d: self._y(d, 0).start())
+
+    def along_b(self):
+        @pl.when(self._owns(self.y))
+        def _():
+            total = self.part[self.y].astype(jnp.float32)
             for d in range(1, Y):
                 self._y_in(d, 0).wait_recv()
-            total = self.part[self.y].astype(jnp.float32)
-            for d in range(1, Y):
                 total = total + self.from_y[mod(self.y + d, Y)].astype(jnp.float32)
             self.sum_y[...] = total.astype(self.sum_y.dtype)
-            self._each_z(lambda d: self._z(d, 0).start())
-
-        when(self._owns(self.y), step)
-
-    def hand_out_z(self, finish):
-        def step():
-            self._each_z(lambda d: self._z_in(d, 0).wait_recv())
-            total = self.sum_y[self.z].astype(jnp.float32)
-            for d in range(1, self.nz):
-                total = total + self.from_z[mod(self.z + d, self.nz)].astype(jnp.float32)
-            self.out[self.y, self.z] = finish(total).astype(self.out.dtype)
-            self._each_z(lambda d: self._z(d, 1).start())
-
-        when(self._owns(self.y), step)
+            for d in range(1, self.nb):
+                self._b(d, 0).start()
+
+    def along_a(self):
+        @pl.when(self._owns(self.y))
+        def _():
+            total = self.sum_y[:, self.b].astype(jnp.float32)
+            for d in range(1, self.nb):
+                self._b(d, 0, True).wait_recv()
+                total = total + self.from_b[mod(self.b + d, self.nb)].astype(jnp.float32)
+            self.sum_b[...] = total.astype(self.sum_b.dtype)
+            for d in range(1, self.na):
+                self._a(d, 0).start()
+
+    def hand_out_a(self, finish):
+        @pl.when(self._owns(self.y))
+        def _():
+            total = self.sum_b[self.a].astype(jnp.float32)
+            for d in range(1, self.na):
+                self._a(d, 0, True).wait_recv()
+                total = total + self.from_a[mod(self.a + d, self.na)].astype(jnp.float32)
+            self.out[self.y, self.a, self.b] = finish(total).astype(self.out.dtype)
+            for d in range(1, self.na):
+                self._a(d, 1).start()
+
+    def hand_out_b(self):
+        @pl.when(self._owns(self.y))
+        def _():
+            for d in range(1, self.na):
+                self._a(d, 1, True).wait_recv()
+            for d in range(1, self.nb):
+                self._b(d, 1).start()
 
     def hand_out_y(self):
-        def step():
-            self._each_z(lambda d: self._z_in(d, 1).wait_recv())
+        @pl.when(self._owns(self.y))
+        def _():
+            for d in range(1, self.nb):
+                self._b(d, 1, True).wait_recv()
             for d in range(1, Y):
                 self._y(d, 1).start()
 
-        when(self._owns(self.y), step)
-
     def end(self):
         for d in range(1, Y):
-            when(self._owns(mod(self.y + d, Y)), lambda: self._y_in(d, 1).wait_recv())
+            pl.when(self._owns(mod(self.y + d, Y)))(lambda d=d: self._y_in(d, 1).wait_recv())
 
     def settle(self):
         for d in range(1, Y):
-            when(self._owns(mod(self.y + d, Y)), lambda: self._y(d, 0).wait_send())
-
-        def mine():
+            pl.when(self._owns(mod(self.y + d, Y)))(lambda d=d: self._y(d, 0).wait_send())
+
+        @pl.when(self._owns(self.y))
+        def _():
             for d in range(1, Y):
                 self._y(d, 1).wait_send()
-
-            def done(d):
-                self._z(d, 0).wait_send()
-                self._z(d, 1).wait_send()
-
-            self._each_z(done)
-
-        when(self._owns(self.y), mine)
+            for give in range(2):
+                for d in range(1, self.nb):
+                    self._b(d, give).wait_send()
+                for d in range(1, self.na):
+                    self._a(d, give).wait_send()
 
 
 class TorusGather:
+    NEAR = 5
+
     @staticmethod
     def scratch(nz):
         return [
-            DMA((2, nz, 2)), DMA((nz, 2)), DMA((3,)), DMA((3,)),
-            DMA((2, nz)), DMA((nz,)), DMA((2, nz)), DMA((2, nz)), DMA((nz,)), DMA((nz,)), DMA((3,)),
+            DMA((1,)), DMA((nz, 2)), DMA((3,)), DMA((3,)),
+            DMA((1,)), DMA((nz,)), DMA((1,)), DMA((2, nz)), DMA((1,)), DMA((2,)), DMA((3,)),
             DMA((2, 2)), DMA((2, 2)), DMA((2,)), DMA((2,)),
         ]
 
@@ -207,28 +227,28 @@
 
     def _a_z(self, origin, p, way):
         block = self._pair(origin, p)
-        self._go(remote(block, block, self.az_s.at[way, origin, p], self.az_r.at[origin, p],
-                        slab=self.next[way] * Y + self.y))
+        remote(block, block, self.az_s.at[0], self.az_r.at[origin, p],
+               slab=self.next[way] * Y + self.y).start()
 
     def _b_z(self, origin, src, way):
-        self._go(remote(src, self.gb.at[origin, self.y], self.bz_s.at[way, origin], self.bz_r.at[origin],
-                        slab=self.next[way] * Y + self.y))
+        remote(src, self.gb.at[origin, self.y], self.bz_s.at[0], self.bz_r.at[origin],
+               slab=self.next[way] * Y + self.y).start()
 
     def _two(self, origin, j):
         return self.gb.at[origin, j, pl.ds(0, 2)]
 
     def _b_y(self, origin, src):
         for way, to in enumerate(self.sides):
-            self._go(remote(src, self._two(origin, self.y), self.by_s.at[way, origin], self.by_r.at[way, origin],
-                            slab=self.z * Y + to))
-
-    def _b_relay(self, origin):
+            remote(src, self._two(origin, self.y), self.by_s.at[0], self.by_r.at[way, origin],
+                   slab=self.z * Y + to).start()
+
+    def _b_relay(self, origin, t):
         self._landed(self._two(origin, self.left), self.by_r.at[0, origin])
         self._landed(self._two(origin, self.right), self.by_r.at[1, origin])
         turn = 1 - 2 * mod(origin, 2)
         block = self._two(origin, mod(self.y - turn + Y, Y))
-        self._go(remote(block, block, self.bo_s.at[origin], self.bo_r.at[origin],
-                        slab=self.z * Y + mod(self.y + turn + Y, Y)))
+        remote(block, block, self.bo_s.at[0], self.bo_r.at[int(t > self.NEAR)],
+               slab=self.z * Y + mod(self.y + turn + Y, Y)).start()
 
     def start(self, meanwhile):
         z, y, wa, wb = self.z, self.y, self.wa, self.wb
@@ -265,26 +285,25 @@
             two = self._two(origin, y)
             self._b_y(origin, two)
             if t == half:
-                self._go(remote(two, two, self.bo_s.at[origin], self.bo_r.at[origin],
-                                slab=self.z * Y + self.across))
+                remote(two, two, self.bo_s.at[0], self.bo_r.at[1],
+                       slab=self.z * Y + self.across).start()
         for p in (y // 2, 1 - y // 2):
             for origin, way, last in ways:
                 self._landed(self._pair(origin, p), self.az_r.at[origin, p])
                 if t < last:
                     self._a_z(origin, p, way)
-        self._b_relay(mod(self.z - t + 1 + nz, nz))
+        self._b_relay(mod(self.z - t + 1 + nz, nz), t - 1)
         if t > 1:
-            self._b_relay(mod(self.z + t - 1, nz))
-
-    def across_landed(self, t):
-        origins = [mod(self.z - t + self.nz, self.nz)]
-        if 0 < t < self.half:
-            origins.append(mod(self.z + t, self.nz))
-        for origin in origins:
-            if t == self.half:
-                self._landed(self._two(origin, self.left), self.by_r.at[0, origin])
-                self._landed(self._two(origin, self.right), self.by_r.at[1, origin])
-            self._landed(self._two(origin, self.across), self.bo_r.at[origin])
+            self._b_relay(mod(self.z + t - 1, nz), t - 1)
+
+    def near_landed(self):
+        self._landed(self.gb.at[pl.ds(0, 2 * self.NEAR + 1), 0, pl.ds(0, 2)], self.bo_r.at[0])
+
+    def far_landed(self):
+        last = mod(self.z + self.half, self.nz)
+        self._landed(self._two(last, self.left), self.by_r.at[0, last])
+        self._landed(self._two(last, self.right), self.by_r.at[1, last])
+        self._landed(self.gb.at[pl.ds(0, self.nz - 2 * self.NEAR - 1), 0, pl.ds(0, 2)], self.bo_r.at[1])
 
     def _late(self, part, j):
         return self.gb.at[self.parts[part], j, 2]
@@ -310,6 +329,14 @@
             self._landed(self._late(way, self.across), self.lo_r.at[way])
 
     def settle(self):
+        nz, one, two = self.nz, pl.ds(0, 1), pl.ds(0, 2)
+        for block, sem in (
+            (self.ga.at[pl.ds(0, nz - 1)], self.az_s),
+            (self.gb.at[pl.ds(0, nz - 1), one], self.bz_s),
+            (self.gb.at[:, two, two], self.by_s),
+            (self.gb.at[:, one, two], self.bo_s),
+        ):
+            remote(block, block, sem.at[0], self.own_sem.at[2], slab=self.z * Y + self.right).wait_send()
         for copy in self.sent:
             copy.wait_send()
 
@@ -339,8 +366,8 @@
     (q, k, v, num, den, num_out, num_in, den_in, attn, live, tsum_part, text_out) = take(12)
     (part, pair, far, near) = take(4)
     qkv = TorusGather(wq, wb, ga, gb, take(QKV_SEMS))
-    text_sum = SlabSum(text_part, text_rows, take(5))
-    attn_sum = SlabSum(tsum_part, text_out, take(5))
+    text_sum = SlabSum(text_part, text_rows, take(8))
+    attn_sum = SlabSum(tsum_part, text_out, take(8))
     q_s, q_r, k_s, k_r, v_s, v_r, n_s, n_r, d_s, d_r = take(10)
     pair_s, pair_r, far_s, far_r, near_s, near_r = take(6)
 
@@ -407,7 +434,7 @@
     aligned = jnp.minimum(slab * depth // LANES * LANES, model - span)
     aligned = pl.multiple_of(aligned, LANES)
     offset = pl.multiple_of(slab * depth - aligned, 16)
-    share = nz // heads
+    na = text_part.shape[1] // heads
 
     def fill_text_weights():
         tweight[...] = jnp.zeros_like(tweight)
@@ -430,7 +457,7 @@
             ).astype(bf16)
             for h in range(heads):
                 block = product[:, h * HEAD_SIZE : (h + 1) * HEAD_SIZE]
-                text_part[i, h * share : (h + 1) * share] = block.reshape(share, txt // share, HEAD_SIZE)
+                text_part[i, h * na : (h + 1) * na] = block.reshape(na, *text_part.shape[2:])
 
     def finish_text(total):
         gain = jnp.where(y == 0, tqg[...], tkg[...])
@@ -447,10 +474,14 @@
             lax.fori_loop(txt // 32, txt // 16, normalize_text, 0)
             multiply_text()
             text_sum.start()
+        if t == 3:
+            text_sum.along_b()
         if t == 4:
-            text_sum.along_z()
+            text_sum.along_a()
+        if t == 6:
+            text_sum.hand_out_a(finish_text)
         if t == 7:
-            text_sum.hand_out_z(finish_text)
+            text_sum.hand_out_b()
         rest = blocks - early
         lax.fori_loop(early + (t - 1) * rest // steps, early + t * rest // steps, normalize_video, 0)
 
@@ -491,12 +522,9 @@
             )
         return carry
 
-    near_steps = 5
-    for t in range(near_steps + 1):
-        qkv.across_landed(t)
+    qkv.near_landed()
     lax.fori_loop(0, 5, multiply_rest, 0)
-    for t in range(near_steps + 1, steps + 1):
-        qkv.across_landed(t)
+    qkv.far_landed()
     lax.fori_loop(5, nz // 2, multiply_rest, 0)
 
     to_right, to_left = [], []
@@ -565,7 +593,7 @@
     text_sum.end()
 
     def text_head(i, h):
-        return text_rows[i, h * share : (h + 1) * share].reshape(txt, HEAD_SIZE)
+        return text_rows[i, h * na : (h + 1) * na].reshape(txt, HEAD_SIZE)
 
     text_values = []
     for h in range(heads):
@@ -575,7 +603,7 @@
         own = scores(text_head(1, h), tq) * live[...] * is_first
         total = weigh(v[0, h], e) + weigh(text_values[h], own)
         tsum_part[h] = total.reshape(tsum_part.shape[1:])
-        tsum_part[heads, 0, h : h + 1] = column_sum(e) + column_sum(own)
+        tsum_part[heads, 0, 0, h : h + 1] = column_sum(e) + column_sum(own)
     attn_sum.start()
 
     live_wide = jnp.concatenate([live[...]] * (tokens // txt), axis=1)
@@ -585,7 +613,7 @@
         den[0, h, 0:1] += column_sum(e)
 
     text_sum.settle()
-    attn_sum.along_z()
+    attn_sum.along_b()
 
     def add_side(slot, tile, h):
         reach = jnp.where(jnp.where(slot == 1, has_left, has_right), 1.0, 0.0)
@@ -623,13 +651,17 @@
         for copy in now:
             copy.start()
         back.append(now)
+        if h == 0:
+            attn_sum.along_a()
+        if h == heads - 1:
+            attn_sum.hand_out_a(lambda total: total)
 
     def own_side(i, carry):
         add_side(1 + i % 2, 0, i // 2)
         return carry
 
     lax.fori_loop(0, 2 * heads, own_side, 0)
-    attn_sum.hand_out_z(lambda total: total)
+    attn_sum.hand_out_b()
     for h in range(heads):
         for copy in back[h]:
             copy.wait_recv()
@@ -713,7 +745,7 @@
 
     attn_sum.end()
     for h in range(heads):
-        total = text_out[h].reshape(HEAD_SIZE, txt) / text_out[heads, 0, h : h + 1]
+        total = text_out[h].reshape(HEAD_SIZE, txt) / text_out[heads, 0, 0, h : h + 1]
         text_final[:, h * HEAD_SIZE : (h + 1) * HEAD_SIZE] = total.T.astype(bf16)
     attn_sum.settle()
     for copy in (*fars, *nears):
@@ -729,8 +761,9 @@
     nz, nx = slab_count // Y, head_count // 2
     rows = tokens // head_count
     bf16, f32 = jnp.bfloat16, jnp.float32
-    text_block = jax.ShapeDtypeStruct((3, nz, txt * heads // nz, HEAD_SIZE), bf16)
-    sum_block = jax.ShapeDtypeStruct((heads + 1, nz, HEAD_SIZE // nz, txt), f32)
+    na = nz // NB
+    text_block = jax.ShapeDtypeStruct((3, na, NB, txt * heads // nz, HEAD_SIZE), bf16)
+    sum_block = jax.ShapeDtypeStruct((heads + 1, na, NB, HEAD_SIZE // nz, txt), f32)
     half = model // 2
     vmem = pl.BlockSpec(memory_space=VMEM)
     return pl.pallas_call(

time: 117 us -> 122 us (1.043)
  the two profiles are of different devices: /device:TPU:6 before, /device:TPU:1 now
where the time goes in v2:
time: 122 us; the launch traced here: 121 us
  Pallas kernels  119 us (98%)
  local copies, waits for them, and re-layouts  1.35 us (1%)
    pallas_call x1, Pallas kernels, run_whole(): pl.pallas_call(whole_kernel, out_shape=(jax.ShapeDtypeStruct((rows, model...  119 us

profile of v2, /device:TPU:1, one launch (start us, length us, event | category | flops | bytes accessed | tf_op | source)
XLA Modules:
  0.0 121.5 jit_solution(17962202461083013579)
XLA Ops:
  0.6 119.5 %whole.1 = (bf16[48,3072]{1,0:T(8,128)(2,1)S(1)}, bf16[128,256]{1,0:T(8,128)(2,1)S(1)}) custom-call(bf16[384,3072]{1,0:T(8,128)(2,1)} %refs_0_.1, bf16[128,3072]{1,0:T(8,128)(2,1)} %refs_1_.1, bf16[48,256]{1,0:T(8,128)(2,1)} %refs_2_.1, bf16[48,256]{1,0:T(8,128)(2,1)} %refs_3_.1, bf16[48,256]{1,0:T(8,128)(2,1)} %refs_4_.1, bf16[48,256]{1,0:T(8,128)(2,1)} %bitcast.7, ...), custom_call_target="tpu_custom_call" | custom-call | tf_op jit(solution)/shard_map/whole/pallas_call | solution.py:769
  120.1 0.7 copy.19
  120.9 0.6 copy.20

commit v3 on v1

--- a/solution.py
+++ b/solution.py
@@ -73,7 +73,7 @@
             VMEM((nz, rows, lanes), block.dtype),
             VMEM((nz, rows, lanes), block.dtype),
             DMA((2, 2, Y)),
-            DMA((2, 2, nz)),
+            DMA((2, 2)),
         ]
 
     def __init__(self, part, out, scratch):
@@ -101,12 +101,12 @@
         z, to = self.z, mod(self.z + d, self.nz)
         src = self.out.at[self.y, z] if give else self.sum_y.at[to]
         dst = self.out.at[self.y, z] if give else self.from_z.at[z]
-        return remote(src, dst, self.zsem.at[give, 0, to], self.zsem.at[give, 1, z], slab=to * Y + self.y)
-
-    def _z_in(self, d, give):
-        of = mod(self.z + d, self.nz)
-        dst = self.out.at[self.y, of] if give else self.from_z.at[of]
-        return remote(dst, dst, self.zsem.at[give, 0, of], self.zsem.at[give, 1, of], slab=of * Y + self.y)
+        return remote(src, dst, self.zsem.at[give, 0], self.zsem.at[give, 1], slab=to * Y + self.y)
+
+    def _all_z(self, give):
+        blocks = self.from_z.at[pl.ds(0, self.nz - 1)]
+        to = mod(self.z + 1, self.nz)
+        return remote(blocks, blocks, self.zsem.at[give, 0], self.zsem.at[give, 1], slab=to * Y + self.y)
 
     def _each_z(self, step):
         def body(d, carry):
@@ -133,7 +133,7 @@
 
     def hand_out_z(self, finish):
         def step():
-            self._each_z(lambda d: self._z_in(d, 0).wait_recv())
+            self._all_z(0).wait_recv()
             total = self.sum_y[self.z].astype(jnp.float32)
             for d in range(1, self.nz):
                 total = total + self.from_z[mod(self.z + d, self.nz)].astype(jnp.float32)
@@ -144,7 +144,7 @@
 
     def hand_out_y(self):
         def step():
-            self._each_z(lambda d: self._z_in(d, 1).wait_recv())
+            self._all_z(1).wait_recv()
             for d in range(1, Y):
                 self._y(d, 1).start()
 
@@ -162,21 +162,21 @@
             for d in range(1, Y):
                 self._y(d, 1).wait_send()
 
-            def done(d):
-                self._z(d, 0).wait_send()
-                self._z(d, 1).wait_send()
-
-            self._each_z(done)
+            self._all_z(0).wait_send()
+            self._all_z(1).wait_send()
 
         when(self._owns(self.y), mine)
 
 
 class TorusGather:
+    RELAYED = 6
+    NEAR = 5
+
     @staticmethod
     def scratch(nz):
         return [
-            DMA((2, nz, 2)), DMA((nz, 2)), DMA((3,)), DMA((3,)),
-            DMA((2, nz)), DMA((nz,)), DMA((2, nz)), DMA((2, nz)), DMA((nz,)), DMA((nz,)), DMA((3,)),
+            DMA((1,)), DMA((nz, 2)), DMA((3,)), DMA((3,)),
+            DMA((1,)), DMA((nz,)), DMA((1,)), DMA((2, nz)), DMA((1,)), DMA((2,)), DMA((3,)),
             DMA((2, 2)), DMA((2, 2)), DMA((2,)), DMA((2,)),
         ]
 
@@ -207,28 +207,28 @@
 
     def _a_z(self, origin, p, way):
         block = self._pair(origin, p)
-        self._go(remote(block, block, self.az_s.at[way, origin, p], self.az_r.at[origin, p],
-                        slab=self.next[way] * Y + self.y))
+        remote(block, block, self.az_s.at[0], self.az_r.at[origin, p],
+               slab=self.next[way] * Y + self.y).start()
 
     def _b_z(self, origin, src, way):
-        self._go(remote(src, self.gb.at[origin, self.y], self.bz_s.at[way, origin], self.bz_r.at[origin],
-                        slab=self.next[way] * Y + self.y))
+        remote(src, self.gb.at[origin, self.y], self.bz_s.at[0], self.bz_r.at[origin],
+               slab=self.next[way] * Y + self.y).start()
 
     def _two(self, origin, j):
         return self.gb.at[origin, j, pl.ds(0, 2)]
 
     def _b_y(self, origin, src):
         for way, to in enumerate(self.sides):
-            self._go(remote(src, self._two(origin, self.y), self.by_s.at[way, origin], self.by_r.at[way, origin],
-                            slab=self.z * Y + to))
-
-    def _b_relay(self, origin):
+            remote(src, self._two(origin, self.y), self.by_s.at[0], self.by_r.at[way, origin],
+                   slab=self.z * Y + to).start()
+
+    def _b_relay(self, origin, t):
         self._landed(self._two(origin, self.left), self.by_r.at[0, origin])
         self._landed(self._two(origin, self.right), self.by_r.at[1, origin])
         turn = 1 - 2 * mod(origin, 2)
         block = self._two(origin, mod(self.y - turn + Y, Y))
-        self._go(remote(block, block, self.bo_s.at[origin], self.bo_r.at[origin],
-                        slab=self.z * Y + mod(self.y + turn + Y, Y)))
+        remote(block, block, self.bo_s.at[0], self.bo_r.at[int(t > self.NEAR)],
+               slab=self.z * Y + mod(self.y + turn + Y, Y)).start()
 
     def start(self, meanwhile):
         z, y, wa, wb = self.z, self.y, self.wa, self.wb
@@ -262,29 +262,37 @@
             self._landed(block, self.bz_r.at[origin])
             if t < last:
                 self._b_z(origin, block, way)
-            two = self._two(origin, y)
-            self._b_y(origin, two)
-            if t == half:
-                self._go(remote(two, two, self.bo_s.at[origin], self.bo_r.at[origin],
-                                slab=self.z * Y + self.across))
+        if t > self.RELAYED:
+            self._along_y(ways, t)
         for p in (y // 2, 1 - y // 2):
             for origin, way, last in ways:
                 self._landed(self._pair(origin, p), self.az_r.at[origin, p])
                 if t < last:
                     self._a_z(origin, p, way)
-        self._b_relay(mod(self.z - t + 1 + nz, nz))
+        if t <= self.RELAYED:
+            self._along_y(ways, t)
         if t > 1:
-            self._b_relay(mod(self.z + t - 1, nz))
-
-    def across_landed(self, t):
-        origins = [mod(self.z - t + self.nz, self.nz)]
-        if 0 < t < self.half:
-            origins.append(mod(self.z + t, self.nz))
-        for origin in origins:
-            if t == self.half:
+            self._b_relay(mod(self.z - t + 2 + nz, nz), t - 2)
+            if t > 2:
+                self._b_relay(mod(self.z + t - 2, nz), t - 2)
+
+    def _along_y(self, ways, t):
+        for origin, _, _ in ways:
+            two = self._two(origin, self.y)
+            self._b_y(origin, two)
+            if t > self.RELAYED:
+                remote(two, two, self.bo_s.at[0], self.bo_r.at[1],
+                       slab=self.z * Y + self.across).start()
+
+    def near_landed(self):
+        self._landed(self.gb.at[pl.ds(0, 2 * self.NEAR + 1), 0, pl.ds(0, 2)], self.bo_r.at[0])
+
+    def far_landed(self):
+        for t in range(self.RELAYED + 1, self.half + 1):
+            for origin in (mod(self.z - t + self.nz, self.nz), mod(self.z + t, self.nz))[: 1 + (t < self.half)]:
                 self._landed(self._two(origin, self.left), self.by_r.at[0, origin])
                 self._landed(self._two(origin, self.right), self.by_r.at[1, origin])
-            self._landed(self._two(origin, self.across), self.bo_r.at[origin])
+        self._landed(self.gb.at[pl.ds(0, self.nz - 2 * self.NEAR - 1), 0, pl.ds(0, 2)], self.bo_r.at[1])
 
     def _late(self, part, j):
         return self.gb.at[self.parts[part], j, 2]
@@ -310,6 +318,14 @@
             self._landed(self._late(way, self.across), self.lo_r.at[way])
 
     def settle(self):
+        nz, one, two = self.nz, pl.ds(0, 1), pl.ds(0, 2)
+        for block, sem in (
+            (self.ga.at[pl.ds(0, nz - 1)], self.az_s),
+            (self.gb.at[pl.ds(0, nz - 1), one], self.bz_s),
+            (self.gb.at[:, two, two], self.by_s),
+            (self.gb.at[:, one, two], self.bo_s),
+        ):
+            remote(block, block, sem.at[0], self.own_sem.at[2], slab=self.z * Y + self.right).wait_send()
         for copy in self.sent:
             copy.wait_send()
 
@@ -430,7 +446,7 @@
             ).astype(bf16)
             for h in range(heads):
                 block = product[:, h * HEAD_SIZE : (h + 1) * HEAD_SIZE]
-                text_part[i, h * share : (h + 1) * share] = block.reshape(share, txt // share, HEAD_SIZE)
+                text_part[i, h * share : (h + 1) * share] = block.reshape(share, *text_part.shape[2:])
 
     def finish_text(total):
         gain = jnp.where(y == 0, tqg[...], tkg[...])
@@ -491,12 +507,9 @@
             )
         return carry
 
-    near_steps = 5
-    for t in range(near_steps + 1):
-        qkv.across_landed(t)
+    qkv.near_landed()
     lax.fori_loop(0, 5, multiply_rest, 0)
-    for t in range(near_steps + 1, steps + 1):
-        qkv.across_landed(t)
+    qkv.far_landed()
     lax.fori_loop(5, nz // 2, multiply_rest, 0)
 
     to_right, to_left = [], []
@@ -584,8 +597,6 @@
         num[0, h] += weigh(text_values[h], e)
         den[0, h, 0:1] += column_sum(e)
 
-    text_sum.settle()
-    attn_sum.along_z()
 
     def add_side(slot, tile, h):
         reach = jnp.where(jnp.where(slot == 1, has_left, has_right), 1.0, 0.0)
@@ -629,7 +640,8 @@
         return carry
 
     lax.fori_loop(0, 2 * heads, own_side, 0)
-    attn_sum.hand_out_z(lambda total: total)
+    attn_sum.along_z()
+    text_sum.settle()
     for h in range(heads):
         for copy in back[h]:
             copy.wait_recv()
@@ -681,7 +693,7 @@
     nears[0].start()
     nears[1].start()
     send_pair(x)
-    attn_sum.hand_out_y()
+    attn_sum.hand_out_z(lambda total: total)
     pair_sum(x)
     fars[0].wait_recv()
     pair[x_right, 0] = (pair[x_right, 0].astype(f32) + far[0].astype(f32)).astype(bf16)
@@ -690,6 +702,7 @@
     pair[x_left, 1] = (pair[x_left, 1].astype(f32) + far[1].astype(f32)).astype(bf16)
     nears[3].start()
     qkv.settle()
+    attn_sum.hand_out_y()
     for copy in (*sum(rows_out, ()), *sum(back, []), *pairs):
         copy.wait_send()
 

time: 117 us -> 109 us (0.932); the launches traced: 115 us -> 109 us
  Pallas kernels: 113 us -> 107 us
    pallas_call x1, Pallas kernels: 113 us -> 107 us  [run_whole(): pl.pallas_call(whole_kernel, out_shape=(jax.ShapeDtypeStruct((rows, model...]
where the time goes in v3:
time: 109 us
  Pallas kernels  107 us (98%)
  local copies, waits for them, and re-layouts  1.35 us (1%)
    pallas_call x1, Pallas kernels, run_whole(): pl.pallas_call(whole_kernel, out_shape=(jax.ShapeDtypeStruct((rows, model...  107 us

profile of v3, /device:TPU:6, one launch (start us, length us, event | category | flops | bytes accessed | tf_op | source)
XLA Modules:
  0.0 109.2 jit_solution(4806864918068913140)
XLA Ops:
  0.6 107.2 %whole.1 = (bf16[48,3072]{1,0:T(8,128)(2,1)S(1)}, bf16[128,256]{1,0:T(8,128)(2,1)S(1)}) custom-call(bf16[384,3072]{1,0:T(8,128)(2,1)} %refs_0_.1, bf16[128,3072]{1,0:T(8,128)(2,1)} %refs_1_.1, bf16[48,256]{1,0:T(8,128)(2,1)} %refs_2_.1, bf16[48,256]{1,0:T(8,128)(2,1)} %refs_3_.1, bf16[48,256]{1,0:T(8,128)(2,1)} %refs_4_.1, bf16[48,256]{1,0:T(8,128)(2,1)} %bitcast.7, ...), custom_call_target="tpu_custom_call" | custom-call | tf_op jit(solution)/shard_map/whole/pallas_call | solution.py:749
  107.8 0.7 copy.19
  108.6 0.6 copy.20

commit v4 on v3

--- a/solution.py
+++ b/solution.py
@@ -297,13 +297,12 @@
     def _late(self, part, j):
         return self.gb.at[self.parts[part], j, 2]
 
-    def late_start(self):
-        for turn in range(2):
-            for way in range(2):
-                part = way if turn == 0 else 1 - way
-                block = self._late(part, self.y)
-                self._go(remote(block, block, self.ly_s.at[way, part], self.ly_r.at[way, part],
-                                slab=self.z * Y + self.sides[way]))
+    def late_start(self, turn):
+        for way in range(2):
+            part = way if turn == 0 else 1 - way
+            block = self._late(part, self.y)
+            self._go(remote(block, block, self.ly_s.at[way, part], self.ly_r.at[way, part],
+                            slab=self.z * Y + self.sides[way]))
 
     def late_relay(self):
         for way in range(2):
@@ -467,11 +466,14 @@
             text_sum.along_z()
         if t == 7:
             text_sum.hand_out_z(finish_text)
-        rest = blocks - early
-        lax.fori_loop(early + (t - 1) * rest // steps, early + t * rest // steps, normalize_video, 0)
+        if t > 2:
+            rest, steps_left = blocks - early, steps - 2
+            lax.fori_loop(
+                early + (t - 3) * rest // steps_left, early + (t - 2) * rest // steps_left, normalize_video, 0
+            )
 
     qkv.own_b.wait()
-    qkv.late_start()
+    qkv.late_start(0)
 
     acc[...] = jnp.zeros_like(acc)
     group = 4 if nz % 4 == 0 else nz
@@ -494,7 +496,6 @@
         to_below.start()
         to_above.start()
         rows_out.append((to_below, to_above))
-    text_sum.hand_out_y()
 
     pair_depth = 2 * Y * depth
 
@@ -511,6 +512,7 @@
     lax.fori_loop(0, 5, multiply_rest, 0)
     qkv.far_landed()
     lax.fori_loop(5, nz // 2, multiply_rest, 0)
+    text_sum.hand_out_y()
 
     to_right, to_left = [], []
     for h in range(heads):
@@ -535,6 +537,8 @@
         pl.when(has_right)(functools.partial(start_all, right_now))
         pl.when(has_left)(functools.partial(start_all, left_now))
 
+    qkv.late_start(1)
+
     @pl.when(jnp.logical_not(has_left))
     def _():
         k[1] = jnp.zeros_like(k[1])
@@ -560,8 +564,6 @@
         num[0, h] = weigh(v[0, h], e)
         den[0, h, 0:1] = column_sum(e)
 
-    qkv.late_relay()
-
     for h in range(heads):
         for copy in rows_out[h]:
             copy.wait_recv()
@@ -573,56 +575,61 @@
             return carry
 
         lax.fori_loop(1, 3, neighbour, 0)
-    live[...] = jnp.broadcast_to(mask[...].astype(f32), live.shape).T
-    is_first = jnp.where(slab == 0, 1.0, 0.0)
-    text_sum.end()
-
-    def text_head(i, h):
-        return text_rows[i, h * share : (h + 1) * share].reshape(txt, HEAD_SIZE)
-
-    text_values = []
-    for h in range(heads):
-        tq = text_head(0, h)
-        text_values.append(text_head(2, h).astype(f32).T.astype(bf16))
-        e = scores(k[0, h], tq)
-        own = scores(text_head(1, h), tq) * live[...] * is_first
-        total = weigh(v[0, h], e) + weigh(text_values[h], own)
-        tsum_part[h] = total.reshape(tsum_part.shape[1:])
-        tsum_part[heads, 0, h : h + 1] = column_sum(e) + column_sum(own)
-    attn_sum.start()
-
-    live_wide = jnp.concatenate([live[...]] * (tokens // txt), axis=1)
-    for h in range(heads):
-        e = scores(text_head(1, h), q[0, h]) * live_wide
-        num[0, h] += weigh(text_values[h], e)
-        den[0, h, 0:1] += column_sum(e)
-
+    qkv.late_relay()
+
+    def has_side(slot):
+        return column != (COLUMN_TILES - 1) * (slot - 1)
 
     def add_side(slot, tile, h):
-        reach = jnp.where(jnp.where(slot == 1, has_left, has_right), 1.0, 0.0)
+        reach = jnp.where(has_side(slot), 1.0, 0.0)
         e = scores(k[slot, h], q[tile, h])
         e = e * (reach * window[1, head * heads + h].astype(f32))
         num[tile, h] += weigh(v[slot, h], e)
         den[tile, h, 0:1] += column_sum(e)
 
+    def text_phase():
+        live[...] = jnp.broadcast_to(mask[...].astype(f32), live.shape).T
+        is_first = jnp.where(slab == 0, 1.0, 0.0)
+        text_sum.end()
+
+        def text_head(i, h):
+            return text_rows[i, h * share : (h + 1) * share].reshape(txt, HEAD_SIZE)
+
+        text_values = []
+        for h in range(heads):
+            tq = text_head(0, h)
+            text_values.append(text_head(2, h).astype(f32).T.astype(bf16))
+            e = scores(k[0, h], tq)
+            own = scores(text_head(1, h), tq) * live[...] * is_first
+            total = weigh(v[0, h], e) + weigh(text_values[h], own)
+            tsum_part[h] = total.reshape(tsum_part.shape[1:])
+            tsum_part[heads, 0, h : h + 1] = column_sum(e) + column_sum(own)
+        attn_sum.start()
+
+        live_wide = jnp.concatenate([live[...]] * (tokens // txt), axis=1)
+        for h in range(heads):
+            e = scores(text_head(1, h), q[0, h]) * live_wide
+            num[0, h] += weigh(text_values[h], e)
+            den[0, h, 0:1] += column_sum(e)
+
     back = []
     for h in range(heads):
 
-        @pl.when(has_left)
-        def _():
-            for sem, dst in ((k_r, k), (v_r, v)):
-                remote(dst.at[1, h], dst.at[1, h], sem.at[0, h], sem.at[0, h], slab=slab - 1).wait_recv()
-
-        @pl.when(has_right)
-        def _():
-            for sem, dst in ((k_r, k), (v_r, v)):
-                remote(dst.at[2, h], dst.at[2, h], sem.at[1, h], sem.at[1, h], slab=slab + 1).wait_recv()
-
-        def side(i, carry, h=h):
-            add_side(1 + i % 2, 1 + i // 2, h)
-            return carry
-
-        lax.fori_loop(0, 4, side, 0)
+        for i in range(2):
+            slot = 1 + mod(i + jump_left.astype(jnp.int32), 2)
+
+            @pl.when(has_side(slot))
+            def _():
+                for sem, dst in ((k_r, k), (v_r, v)):
+                    block = dst.at[slot, h]
+                    arrived = sem.at[slot - 1, h]
+                    remote(block, block, arrived, arrived, slab=slab + 2 * slot - 3).wait_recv()
+
+            def side(tile, carry, h=h, slot=slot):
+                add_side(slot, tile, h)
+                return carry
+
+            lax.fori_loop(1, 3, side, 0)
         for tile in (1, 2):
             num_out[tile - 1, h] = num[tile, h].astype(bf16)
         now = [
@@ -634,6 +641,8 @@
         for copy in now:
             copy.start()
         back.append(now)
+        if h == 0:
+            text_phase()
 
     def own_side(i, carry):
         add_side(1 + i % 2, 0, i // 2)

time: 109 us -> 109 us (level)
  no operation moved by 1% of the time
where the time goes in v4:
time: 109 us; the launch traced here: 108 us
  Pallas kernels  106 us (97%)
  local copies, waits for them, and re-layouts  1.35 us (1%)
    pallas_call x1, Pallas kernels, run_whole(): pl.pallas_call(whole_kernel, out_shape=(jax.ShapeDtypeStruct((rows, model...  106 us

profile of v4, /device:TPU:6, one launch (start us, length us, event | category | flops | bytes accessed | tf_op | source)
XLA Modules:
  0.0 108.4 jit_solution(10914429205279292731)
XLA Ops:
  0.6 106.4 %whole.1 = (bf16[48,3072]{1,0:T(8,128)(2,1)S(1)}, bf16[128,256]{1,0:T(8,128)(2,1)S(1)}) custom-call(bf16[384,3072]{1,0:T(8,128)(2,1)} %refs_0_.1, bf16[128,3072]{1,0:T(8,128)(2,1)} %refs_1_.1, bf16[48,256]{1,0:T(8,128)(2,1)} %refs_2_.1, bf16[48,256]{1,0:T(8,128)(2,1)} %refs_3_.1, bf16[48,256]{1,0:T(8,128)(2,1)} %refs_4_.1, bf16[48,256]{1,0:T(8,128)(2,1)} %bitcast.7, ...), custom_call_target="tpu_custom_call" | custom-call | tf_op jit(solution)/shard_map/whole/pallas_call | solution.py:758
  107.0 0.7 copy.19
  107.8 0.6 copy.20

commit v5 on v4

--- a/solution.py
+++ b/solution.py
@@ -376,7 +376,7 @@
     heads = width // HEAD_SIZE
     tokens, model = video.shape
     txt = text.shape[0]
-    score_scale = 1.0 / math.sqrt(HEAD_SIZE)
+    score_scale = math.log2(math.e) / math.sqrt(HEAD_SIZE)
     steps = nz // 2
     nt = (((1,), (1,)), ((), ()))
 
@@ -499,44 +499,48 @@
 
     pair_depth = 2 * Y * depth
 
-    def multiply_rest(i, carry):
+    def multiply_rest(i, j):
         at = mod(z // 2 + i + nz // 2 - 2, nz // 2)
         rows = normed[:, pl.ds(pl.multiple_of(at * pair_depth, pair_depth), pair_depth)]
-        for j in range(2):
-            acc[:, (j + 1) * width : (j + 2) * width] += jnp.dot(
-                rows, gb[pl.ds(at * 2, 2), :, j].reshape(pair_depth, width), preferred_element_type=f32
-            )
-        return carry
+        acc[:, (j + 1) * width : (j + 2) * width] += jnp.dot(
+            rows, gb[pl.ds(at * 2, 2), :, j].reshape(pair_depth, width), preferred_element_type=f32
+        )
+
+    def multiply_pairs(first, last, j):
+        def body(i, carry):
+            multiply_rest(i, j)
+            return carry
+
+        lax.fori_loop(first, last, body, 0)
 
     qkv.near_landed()
-    lax.fori_loop(0, 5, multiply_rest, 0)
+    multiply_pairs(0, 5, 0)
+    multiply_pairs(0, 5, 1)
     qkv.far_landed()
-    lax.fori_loop(5, nz // 2, multiply_rest, 0)
+    multiply_pairs(5, nz // 2, 0)
     text_sum.hand_out_y()
 
     to_right, to_left = [], []
+
+    def send_sides(block, send, arrived, h):
+        right_now = remote(block.at[0, h], block.at[1, h], send.at[0, h], arrived.at[0, h], slab=slab + 1)
+        left_now = remote(block.at[0, h], block.at[2, h], send.at[1, h], arrived.at[1, h], slab=slab - 1)
+        pl.when(has_right)(right_now.start)
+        pl.when(has_left)(left_now.start)
+        to_right.append(right_now)
+        to_left.append(left_now)
+
     for h in range(heads):
         values = acc[:, width + h * HEAD_SIZE : width + (h + 1) * HEAD_SIZE]
         k[0, h] = (values * row_scale(values) * kg[...]).astype(bf16)
+        if h == 0:
+            send_sides(k, k_s, k_r, h)
+    multiply_pairs(5, nz // 2, 1)
+    for h in range(heads):
         v[0, h] = acc[:, 2 * width + h * HEAD_SIZE : 2 * width + (h + 1) * HEAD_SIZE].T.astype(bf16)
-        right_now = [
-            remote(k.at[0, h], k.at[1, h], k_s.at[0, h], k_r.at[0, h], slab=slab + 1),
-            remote(v.at[0, h], v.at[1, h], v_s.at[0, h], v_r.at[0, h], slab=slab + 1),
-        ]
-        left_now = [
-            remote(k.at[0, h], k.at[2, h], k_s.at[1, h], k_r.at[1, h], slab=slab - 1),
-            remote(v.at[0, h], v.at[2, h], v_s.at[1, h], v_r.at[1, h], slab=slab - 1),
-        ]
-        to_right += right_now
-        to_left += left_now
-
-        def start_all(copies):
-            for copy in copies:
-                copy.start()
-
-        pl.when(has_right)(functools.partial(start_all, right_now))
-        pl.when(has_left)(functools.partial(start_all, left_now))
-
+        if h > 0:
+            send_sides(k, k_s, k_r, h)
+        send_sides(v, v_s, v_r, h)
     qkv.late_start(1)
 
     @pl.when(jnp.logical_not(has_left))
@@ -550,7 +554,7 @@
         v[2] = jnp.zeros_like(v[2])
 
     def scores(keys, queries):
-        return jnp.exp(lax.dot_general(keys, queries, nt, preferred_element_type=f32) * score_scale)
+        return jnp.exp2(lax.dot_general(keys, queries, nt, preferred_element_type=f32) * score_scale)
 
     def weigh(values, e):
         return jnp.dot(values, e.astype(bf16), preferred_element_type=f32)
@@ -581,11 +585,10 @@
         return column != (COLUMN_TILES - 1) * (slot - 1)
 
     def add_side(slot, tile, h):
-        reach = jnp.where(has_side(slot), 1.0, 0.0)
+        reach = jnp.where(has_side(slot), 1.0, 0.0) * window[1, head * heads + h].astype(f32)
         e = scores(k[slot, h], q[tile, h])
-        e = e * (reach * window[1, head * heads + h].astype(f32))
-        num[tile, h] += weigh(v[slot, h], e)
-        den[tile, h, 0:1] += column_sum(e)
+        num[tile, h] += weigh(v[slot, h], e) * reach
+        den[tile, h, 0:1] += column_sum(e) * reach
 
     def text_phase():
         live[...] = jnp.broadcast_to(mask[...].astype(f32), live.shape).T
@@ -662,7 +665,6 @@
         attn[:, h * HEAD_SIZE : (h + 1) * HEAD_SIZE] = (total / under).T.astype(bf16)
 
     qkv.late_end()
-    order = (x_far, x_right, x_left, x)
     rows = tokens // nx
     halves = part.shape[2]
     pairs = []
@@ -674,36 +676,43 @@
             product = lax.dot_general(mine, weight, nt, preferred_element_type=f32).astype(bf16)
             for c in range(2):
                 part[xx, c, half] = product[c * rows // 2 : (c + 1) * rows // 2]
-        pairs.append(remote(part.at[xx, 1 - core], pair.at[xx], pair_s.at[xx], pair_r.at[xx], head=other))
-        pairs[-1].start()
-
-    def pair_sum(xx):
-        remote(pair.at[xx], pair.at[xx], pair_s.at[xx], pair_r.at[xx], head=other).wait_recv()
-        pair[xx] = (pair[xx].astype(f32) + part[xx, core].astype(f32)).astype(bf16)
-
-    send_pair(x_far)
-    send_pair(x_right)
-    send_pair(x_left)
-    pair_sum(x_far)
+            pairs.append(
+                remote(part.at[xx, 1 - core, half], pair.at[xx, half], pair_s.at[xx, half], pair_r.at[xx, half],
+                       head=other)
+            )
+            pairs[-1].start()
+
+    def pair_sum(xx, half):
+        block = pair.at[xx, half]
+        remote(block, block, pair_s.at[xx, half], pair_r.at[xx, half], head=other).wait_recv()
+        pair[xx, half] = (pair[xx, half].astype(f32) + part[xx, core, half].astype(f32)).astype(bf16)
+
     fars = [
         remote(pair.at[x_far, 0], far.at[0], far_s.at[0], far_r.at[0], head=right),
         remote(pair.at[x_far, 1], far.at[1], far_s.at[1], far_r.at[1], head=left),
     ]
-    for copy in fars:
-        copy.start()
-    pair_sum(x_right)
-    pair_sum(x_left)
+    send_pair(x_far)
+    send_pair(x_right)
+    for half in range(halves):
+        pair_sum(x_far, half)
+        fars[half].start()
+    send_pair(x_left)
     nears = [
         remote(pair.at[x_right, 1], near.at[0, 1], near_s.at[0, 1], near_r.at[0, 1], head=right),
         remote(pair.at[x_left, 0], near.at[1, 0], near_s.at[1, 0], near_r.at[1, 0], head=left),
         remote(pair.at[x_right, 0], near.at[0, 0], near_s.at[0, 0], near_r.at[0, 0], head=right),
         remote(pair.at[x_left, 1], near.at[1, 1], near_s.at[1, 1], near_r.at[1, 1], head=left),
     ]
+    pair_sum(x_right, 1)
     nears[0].start()
+    pair_sum(x_left, 0)
     nears[1].start()
+    pair_sum(x_right, 0)
+    pair_sum(x_left, 1)
     send_pair(x)
     attn_sum.hand_out_z(lambda total: total)
-    pair_sum(x)
+    for half in range(halves):
+        pair_sum(x, half)
     fars[0].wait_recv()
     pair[x_right, 0] = (pair[x_right, 0].astype(f32) + far[0].astype(f32)).astype(bf16)
     nears[2].start()
@@ -796,7 +805,7 @@
             *SlabSum.scratch(text_block),
             *SlabSum.scratch(sum_block),
             *[DMA((2, heads))] * 10,
-            DMA((nx,)), DMA((nx,)), DMA((2,)), DMA((2,)), DMA((2, 2)), DMA((2, 2)),
+            DMA((nx, 2)), DMA((nx, 2)), DMA((2,)), DMA((2,)), DMA((2, 2)), DMA((2, 2)),
         ],
         compiler_params=pltpu.CompilerParams(
             collective_id=0, has_side_effects=True, vmem_limit_bytes=32 * MIB

time: 109 us -> 109 us (level)
  no operation moved by 1% of the time
where the time goes in v5:
time: 109 us
  Pallas kernels  107 us (98%)
  local copies, waits for them, and re-layouts  1.35 us (1%)
    pallas_call x1, Pallas kernels, run_whole(): pl.pallas_call(whole_kernel, out_shape=(jax.ShapeDtypeStruct((rows, model...  107 us

profile of v5, /device:TPU:6, one launch (start us, length us, event | category | flops | bytes accessed | tf_op | source)
XLA Modules:
  0.0 108.5 jit_solution(1601455058235600470)
XLA Ops:
  0.6 106.5 %whole.1 = (bf16[48,3072]{1,0:T(8,128)(2,1)S(1)}, bf16[128,256]{1,0:T(8,128)(2,1)S(1)}) custom-call(bf16[384,3072]{1,0:T(8,128)(2,1)} %refs_0_.1, bf16[128,3072]{1,0:T(8,128)(2,1)} %refs_1_.1, bf16[48,256]{1,0:T(8,128)(2,1)} %refs_2_.1, bf16[48,256]{1,0:T(8,128)(2,1)} %refs_3_.1, bf16[48,256]{1,0:T(8,128)(2,1)} %refs_4_.1, bf16[48,256]{1,0:T(8,128)(2,1)} %bitcast.7, ...), custom_call_target="tpu_custom_call" | custom-call | tf_op jit(solution)/shard_map/whole/pallas_call | solution.py:767
  107.2 0.7 copy.19
  107.9 0.6 copy.20

commit v6 on v5

--- a/solution.py
+++ b/solution.py
@@ -473,7 +473,6 @@
             )
 
     qkv.own_b.wait()
-    qkv.late_start(0)
 
     acc[...] = jnp.zeros_like(acc)
     group = 4 if nz % 4 == 0 else nz
@@ -541,6 +540,7 @@
         if h > 0:
             send_sides(k, k_s, k_r, h)
         send_sides(v, v_s, v_r, h)
+    qkv.late_start(0)
     qkv.late_start(1)
 
     @pl.when(jnp.logical_not(has_left))
@@ -579,8 +579,6 @@
             return carry
 
         lax.fori_loop(1, 3, neighbour, 0)
-    qkv.late_relay()
-
     def has_side(slot):
         return column != (COLUMN_TILES - 1) * (slot - 1)
 
@@ -646,13 +644,13 @@
         back.append(now)
         if h == 0:
             text_phase()
+    qkv.late_relay()
 
     def own_side(i, carry):
         add_side(1 + i % 2, 0, i // 2)
         return carry
 
     lax.fori_loop(0, 2 * heads, own_side, 0)
-    attn_sum.along_z()
     text_sum.settle()
     for h in range(heads):
         for copy in back[h]:
@@ -693,6 +691,7 @@
     ]
     send_pair(x_far)
     send_pair(x_right)
+    attn_sum.along_z()
     for half in range(halves):
         pair_sum(x_far, half)
         fars[half].start()

time: 109 us -> 110 us (level)
    pallas_call x1, Pallas kernels: 107 us -> 108 us  [run_whole(): pl.pallas_call(whole_kernel, out_shape=(jax.ShapeDtypeStruct((rows, model...]
where the time goes in v6:
time: 110 us
  Pallas kernels  108 us (98%)
  local copies, waits for them, and re-layouts  1.35 us (1%)
    pallas_call x1, Pallas kernels, run_whole(): pl.pallas_call(whole_kernel, out_shape=(jax.ShapeDtypeStruct((rows, model...  108 us

profile of v6, /device:TPU:6, one launch (start us, length us, event | category | flops | bytes accessed | tf_op | source)
XLA Modules:
  0.0 109.7 jit_solution(7912631752739800644)
XLA Ops:
  0.6 107.7 %whole.1 = (bf16[48,3072]{1,0:T(8,128)(2,1)S(1)}, bf16[128,256]{1,0:T(8,128)(2,1)S(1)}) custom-call(bf16[384,3072]{1,0:T(8,128)(2,1)} %refs_0_.1, bf16[128,3072]{1,0:T(8,128)(2,1)} %refs_1_.1, bf16[48,256]{1,0:T(8,128)(2,1)} %refs_2_.1, bf16[48,256]{1,0:T(8,128)(2,1)} %refs_3_.1, bf16[48,256]{1,0:T(8,128)(2,1)} %refs_4_.1, bf16[48,256]{1,0:T(8,128)(2,1)} %bitcast.7, ...), custom_call_target="tpu_custom_call" | custom-call | tf_op jit(solution)/shard_map/whole/pallas_call | solution.py:766
  108.3 0.7 copy.19
  109.0 0.6 copy.20

commit v7 on v5

--- a/solution.py
+++ b/solution.py
@@ -518,7 +518,6 @@
     multiply_pairs(0, 5, 1)
     qkv.far_landed()
     multiply_pairs(5, nz // 2, 0)
-    text_sum.hand_out_y()
 
     to_right, to_left = [], []
 
@@ -541,6 +540,7 @@
         if h > 0:
             send_sides(k, k_s, k_r, h)
         send_sides(v, v_s, v_r, h)
+    text_sum.hand_out_y()
     qkv.late_start(1)
 
     @pl.when(jnp.logical_not(has_left))
@@ -644,15 +644,14 @@
         for copy in now:
             copy.start()
         back.append(now)
-        if h == 0:
-            text_phase()
+
+    text_phase()
 
     def own_side(i, carry):
         add_side(1 + i % 2, 0, i // 2)
         return carry
 
     lax.fori_loop(0, 2 * heads, own_side, 0)
-    attn_sum.along_z()
     text_sum.settle()
     for h in range(heads):
         for copy in back[h]:
@@ -693,6 +692,7 @@
     ]
     send_pair(x_far)
     send_pair(x_right)
+    attn_sum.along_z()
     for half in range(halves):
         pair_sum(x_far, half)
         fars[half].start()

time: 109 us -> 109 us (level)
  no operation moved by 1% of the time
where the time goes in v7:
time: 109 us; the launch traced here: 108 us
  Pallas kernels  106 us (97%)
  local copies, waits for them, and re-layouts  1.35 us (1%)
    pallas_call x1, Pallas kernels, run_whole(): pl.pallas_call(whole_kernel, out_shape=(jax.ShapeDtypeStruct((rows, model...  106 us

profile of v7, /device:TPU:6, one launch (start us, length us, event | category | flops | bytes accessed | tf_op | source)
XLA Modules:
  0.0 108.5 jit_solution(1456760629929427746)
XLA Ops:
  0.6 106.5 %whole.1 = (bf16[48,3072]{1,0:T(8,128)(2,1)S(1)}, bf16[128,256]{1,0:T(8,128)(2,1)S(1)}) custom-call(bf16[384,3072]{1,0:T(8,128)(2,1)} %refs_0_.1, bf16[128,3072]{1,0:T(8,128)(2,1)} %refs_1_.1, bf16[48,256]{1,0:T(8,128)(2,1)} %refs_2_.1, bf16[48,256]{1,0:T(8,128)(2,1)} %refs_3_.1, bf16[48,256]{1,0:T(8,128)(2,1)} %refs_4_.1, bf16[48,256]{1,0:T(8,128)(2,1)} %bitcast.7, ...), custom_call_target="tpu_custom_call" | custom-call | tf_op jit(solution)/shard_map/whole/pallas_call | solution.py:767
  107.1 0.7 copy.19
  107.8 0.6 copy.20

commit v8 on v7

--- a/solution.py
+++ b/solution.py
@@ -709,16 +709,14 @@
     nears[1].start()
     pair_sum(x_right, 0)
     pair_sum(x_left, 1)
-    send_pair(x)
     attn_sum.hand_out_z(lambda total: total)
-    for half in range(halves):
-        pair_sum(x, half)
     fars[0].wait_recv()
     pair[x_right, 0] = (pair[x_right, 0].astype(f32) + far[0].astype(f32)).astype(bf16)
     nears[2].start()
     fars[1].wait_recv()
     pair[x_left, 1] = (pair[x_left, 1].astype(f32) + far[1].astype(f32)).astype(bf16)
     nears[3].start()
+    send_pair(x)
     qkv.settle()
     attn_sum.hand_out_y()
     for copy in (*sum(rows_out, ()), *sum(back, []), *pairs):
@@ -734,6 +732,8 @@
         for copy in to_left:
             copy.wait_send()
 
+    for half in range(halves):
+        pair_sum(x, half)
     for copy in nears:
         copy.wait_recv()
     for half in range(halves):

time: 109 us -> 109 us (level)
  no operation moved by 1% of the time
where the time goes in v8:
time: 109 us; the launch traced here: 108 us
  Pallas kernels  106 us (97%)
  local copies, waits for them, and re-layouts  1.35 us (1%)
    pallas_call x1, Pallas kernels, run_whole(): pl.pallas_call(whole_kernel, out_shape=(jax.ShapeDtypeStruct((rows, model...  106 us

profile of v8, /device:TPU:6, one launch (start us, length us, event | category | flops | bytes accessed | tf_op | source)
XLA Modules:
  0.0 108.5 jit_solution(11311959947972649706)
XLA Ops:
  0.6 106.5 %whole.1 = (bf16[48,3072]{1,0:T(8,128)(2,1)S(1)}, bf16[128,256]{1,0:T(8,128)(2,1)S(1)}) custom-call(bf16[384,3072]{1,0:T(8,128)(2,1)} %refs_0_.1, bf16[128,3072]{1,0:T(8,128)(2,1)} %refs_1_.1, bf16[48,256]{1,0:T(8,128)(2,1)} %refs_2_.1, bf16[48,256]{1,0:T(8,128)(2,1)} %refs_3_.1, bf16[48,256]{1,0:T(8,128)(2,1)} %refs_4_.1, bf16[48,256]{1,0:T(8,128)(2,1)} %bitcast.7, ...), custom_call_target="tpu_custom_call" | custom-call | tf_op jit(solution)/shard_map/whole/pallas_call | solution.py:767
  107.1 0.7 copy.19
  107.8 0.6 copy.20
